TPU v7x, 512 devices: a whole 4x4x16 slice. The times are simulated.
512 devices in a mesh: seq: 64 (over z, x), kv: 8 (over y, core).
Axes of the slice: x: 4, y: 4, z: 16, core: 2. Of those that a mesh axis runs over, the one named last changes fastest.
Arguments:
- queries: bfloat16 [16384, 8192], P(('seq', 'kv')), may hold values from -5 to 5
- keys: bfloat16 [16384, 1024], P(('seq', 'kv')), may hold values from -5 to 5
- values: bfloat16 [16384, 1024], P(('seq', 'kv')), may hold values from -6 to 6
- grad_out: bfloat16 [16384, 8192], P(('seq', 'kv')), may hold values from -6 to 6
- lengths: int32 [32], replicated, may hold values from 1 to 1536, 16384 in all
Outputs:
- attended: bfloat16 [16384, 8192], P(('seq', 'kv'))
- grad_queries: bfloat16 [16384, 8192], P(('seq', 'kv'))
- grad_keys: bfloat16 [16384, 1024], P(('seq', 'kv'))
- grad_values: bfloat16 [16384, 1024], P(('seq', 'kv'))
Inputs may be any that keep to these rules, and one draw needn't show every extreme that they name: lengths sum to 16384; the longest is exactly 1536.
All inputs are finite; a program needn't handle non-finite values.
Results may differ from a plain program's by a relative error of at most 0.025.
Values may be sent and summed in bfloat16 or wider, within the bound.
A program may use at most 64 MiB of HBM per device.

v0:
```python
import jax
import jax.numpy as jnp
from jax import lax
from jax.sharding import PartitionSpec as P

HD = 128
GROUP = 8
WIN = 6


def from_behind(value, axis, by):
    peers = lax.axis_size(axis)
    pairs = [(i, i + by) for i in range(peers) if 0 <= i + by < peers]
    return lax.ppermute(value, axis, pairs)


def segment_of(positions, ends):
    counted = jnp.sum((positions[:, None] >= ends[None, :]).astype(jnp.int32), axis=1)
    return jnp.where(positions >= 0, counted, -1)


def body(queries, keys, values, grad_out, lengths):
    query_loc, key_loc, val_loc, grad_loc = (
        lax.all_to_all(queries, "kv", split_axis=1, concat_axis=0, tiled=True),
        lax.all_to_all(keys, "kv", split_axis=1, concat_axis=0, tiled=True),
        lax.all_to_all(values, "kv", split_axis=1, concat_axis=0, tiled=True),
        lax.all_to_all(grad_out, "kv", split_axis=1, concat_axis=0, tiled=True),
    )
    row_count = query_loc.shape[0]
    softmax_scale = HD ** (-0.5)
    window = (WIN + 1) * row_count
    key_pieces = [key_loc]
    val_pieces = [val_loc]
    for distance in range(1, WIN + 1):
        key_far, val_far = from_behind((key_loc, val_loc), "seq", distance)
        key_pieces.insert(0, key_far)
        val_pieces.insert(0, val_far)
    key_win = jnp.concatenate(key_pieces, axis=0)
    val_win = jnp.concatenate(val_pieces, axis=0)
    ends = jnp.cumsum(lengths)
    first_pos = lax.axis_index("seq") * row_count
    query_pos = first_pos + jnp.arange(row_count, dtype=jnp.int32)
    key_pos = first_pos - WIN * row_count + jnp.arange(window, dtype=jnp.int32)
    allowed = (
        (segment_of(key_pos, ends)[None, :] == segment_of(query_pos, ends)[:, None])
        & (key_pos[None, :] <= query_pos[:, None])
        & (key_pos[None, :] >= 0)
    )
    allowed_pair = jnp.tile(allowed, (2, 1))
    query_pairs = (
        query_loc.reshape(row_count, GROUP, HD)
        .transpose(1, 0, 2)
        .reshape(GROUP // 2, 2 * row_count, HD)
    )
    grad_pairs = (
        grad_loc.reshape(row_count, GROUP, HD)
        .transpose(1, 0, 2)
        .reshape(GROUP // 2, 2 * row_count, HD)
    )

    def pair_step(carry, inputs):
        key_acc, val_acc = carry
        query_rows, grad_rows = inputs
        scores = jnp.dot(query_rows, key_win.T, preferred_element_type=jnp.float32) * softmax_scale
        scores = jnp.where(allowed_pair, scores, -jnp.inf)
        row_max = jnp.max(scores, axis=-1, keepdims=True)
        log_total = row_max + jnp.log(jnp.sum(jnp.exp(scores - row_max), axis=-1, keepdims=True))
        weights = jnp.where(allowed_pair, jnp.exp(scores - log_total), 0.0)
        weights_low = weights.astype(jnp.bfloat16)
        attended = jnp.dot(weights_low, val_win, preferred_element_type=jnp.float32).astype(
            jnp.bfloat16
        )
        delta = jnp.sum(grad_rows.astype(jnp.float32) * attended.astype(jnp.float32), axis=-1)
        grad_weights = jnp.dot(grad_rows, val_win.T, preferred_element_type=jnp.float32)
        grad_low = (weights * (grad_weights - delta[:, None])).astype(jnp.bfloat16)
        grad_query = (
            softmax_scale * jnp.dot(grad_low, key_win, preferred_element_type=jnp.float32)
        ).astype(jnp.bfloat16)
        key_acc = key_acc + jnp.dot(grad_low.T, query_rows, preferred_element_type=jnp.float32)
        val_acc = val_acc + jnp.dot(weights_low.T, grad_rows, preferred_element_type=jnp.float32)
        return ((key_acc, val_acc), (attended, grad_query))

    zeros_init = jnp.zeros((window, HD), jnp.float32)
    (key_acc, val_acc), (attended, grad_query) = lax.scan(
        pair_step, (zeros_init, zeros_init), (query_pairs, grad_pairs)
    )
    attended = (
        attended.reshape(GROUP, row_count, HD).transpose(1, 0, 2).reshape(row_count, GROUP * HD)
    )
    grad_query = (
        grad_query.reshape(GROUP, row_count, HD).transpose(1, 0, 2).reshape(row_count, GROUP * HD)
    )
    key_stack = key_acc.reshape(WIN + 1, row_count, HD)[::-1]
    val_stack = val_acc.reshape(WIN + 1, row_count, HD)[::-1]
    key_total = key_stack[0]
    val_total = val_stack[0]
    for distance in range(1, WIN + 1):
        key_back, val_back = from_behind(
            (key_stack[distance], val_stack[distance]), "seq", -distance
        )
        key_total = key_total + key_back
        val_total = val_total + val_back
    grad_keys = (softmax_scale * key_total).astype(jnp.bfloat16)
    grad_values = val_total.astype(jnp.bfloat16)
    return (
        lax.all_to_all(attended, "kv", split_axis=0, concat_axis=1, tiled=True),
        lax.all_to_all(grad_query, "kv", split_axis=0, concat_axis=1, tiled=True),
        lax.all_to_all(grad_keys, "kv", split_axis=0, concat_axis=1, tiled=True),
        lax.all_to_all(grad_values, "kv", split_axis=0, concat_axis=1, tiled=True),
    )


def solution(mesh):
    placed = (
        P(("seq", "kv"), None),
        P(("seq", "kv"), None),
        P(("seq", "kv"), None),
        P(("seq", "kv"), None),
        P(),
    )
    return jax.shard_map(
        body,
        mesh=mesh,
        in_specs=placed,
        out_specs=(
            P(("seq", "kv"), None),
            P(("seq", "kv"), None),
            P(("seq", "kv"), None),
            P(("seq", "kv"), None),
        ),
        check_vma=False,
    )
```

profile of v0, /device:TPU:100, one launch (start us, length us, event | category | flops | bytes accessed | tf_op | source)
XLA Modules:
  0.0 268.4 jit_solution(1916032675527525064)
XLA Ops:
  2.1 4.5 %all-to-all-start.1 = ((bf16[32,8,128]{2,0,1:T(8,128)(2,1)}), bf16[32,8,128]{2,0,1:T(8,128)(2,1)S(1)}, u32[]{:S(2)}, u32[]{:S(2)}) async-start(bf16[32,8,128]{2,0,1:T(8,128)(2,1)} %copy_bitcast_fusion.6), calls=%async_computation.1 | async-start | bytes 131072 | tf_op jit(solution)/shard_map/all_to_all | solution.py:25
  9.2 3.0 %all-to-all-done.1 = bf16[32,8,128]{2,0,1:T(8,128)(2,1)S(1)} async-done(((bf16[32,8,128]{2,0,1:T(8,128)(2,1)}), bf16[32,8,128]{2,0,1:T(8,128)(2,1)S(1)}, u32[]{:S(2)}, u32[]{:S(2)}) %all-to-all-start.1) | async-done | bytes 65568 | tf_op jit(solution)/shard_map/all_to_all | solution.py:25
  12.2 3.4 %all-to-all-start.3 = ((bf16[32,8,128]{2,0,1:T(8,128)(2,1)}), bf16[32,8,128]{2,0,1:T(8,128)(2,1)S(1)}, u32[]{:S(2)}, u32[]{:S(2)}) async-start(bf16[32,8,128]{2,0,1:T(8,128)(2,1)} %copy_bitcast_fusion.5), calls=%async_computation.3 | async-start | bytes 131072 | tf_op jit(solution)/shard_map/all_to_all | solution.py:26
  15.6 6.4 %collective-permute-start = (bf16[256,128]{1,0:T(8,128)(2,1)S(1)}, bf16[256,128]{1,0:T(8,128)(2,1)S(1)}, u32[]{:S(2)}, u32[]{:S(2)}) collective-permute-start(bf16[256,128]{1,0:T(8,128)(2,1)S(1)} %bitcast.153), channel_id=1, source_target_pairs={{0,48},{8,56},{16,64},{24,72},{32,80},{40,88},{48,96},{56,104},{64... | collective-permute-start | bytes 196616 | tf_op jit(solution)/shard_map/ppermute | solution.py:14
  22.5 1.9 copy.111
  26.3 5.3 %collective-permute-start.1 = (bf16[256,128]{1,0:T(8,128)(2,1)S(1)}, bf16[256,128]{1,0:T(8,128)(2,1)S(1)}, u32[]{:S(2)}, u32[]{:S(2)}) collective-permute-start(bf16[256,128]{1,0:T(8,128)(2,1)S(1)} %bitcast.154), channel_id=1, source_target_pairs={{0,40},{8,48},{16,56},{24,64},{32,72},{40,80},{48,88},{56,96},{64,... | collective-permute-start | bytes 196616 | tf_op jit(solution)/shard_map/ppermute | solution.py:14
  31.6 3.8 %collective-permute-start.2 = (bf16[256,128]{1,0:T(8,128)(2,1)S(1)}, bf16[256,128]{1,0:T(8,128)(2,1)S(1)}, u32[]{:S(2)}, u32[]{:S(2)}) collective-permute-start(bf16[256,128]{1,0:T(8,128)(2,1)S(1)} %bitcast.155), channel_id=1, source_target_pairs={{0,32},{8,40},{16,48},{24,56},{32,64},{40,72},{48,80},{56,88},{64,... | collective-permute-start | bytes 196616 | tf_op jit(solution)/shard_map/ppermute | solution.py:14
  35.5 4.4 %collective-permute-start.3 = (bf16[256,128]{1,0:T(8,128)(2,1)S(1)}, bf16[256,128]{1,0:T(8,128)(2,1)S(1)}, u32[]{:S(2)}, u32[]{:S(2)}) collective-permute-start(bf16[256,128]{1,0:T(8,128)(2,1)S(1)} %bitcast.156), channel_id=1, source_target_pairs={{0,24},{8,32},{16,40},{24,48},{32,56},{40,64},{48,72},{56,80},{64,... | collective-permute-start | bytes 196616 | tf_op jit(solution)/shard_map/ppermute | solution.py:14
  39.9 6.1 %collective-permute-start.4 = (bf16[256,128]{1,0:T(8,128)(2,1)S(1)}, bf16[256,128]{1,0:T(8,128)(2,1)S(1)}, u32[]{:S(2)}, u32[]{:S(2)}) collective-permute-start(bf16[256,128]{1,0:T(8,128)(2,1)S(1)} %bitcast.157), channel_id=1, source_target_pairs={{0,16},{8,24},{16,32},{24,40},{32,48},{40,56},{48,64},{56,72},{64,... | collective-permute-start | bytes 196616 | tf_op jit(solution)/shard_map/ppermute | solution.py:14
  46.1 1.9 collective-permute-start.5
  48.6 4.7 %all-to-all-start = ((bf16[32,8,1024]{2,0,1:T(8,128)(2,1)}), bf16[32,8,1024]{2,0,1:T(8,128)(2,1)S(1)}, u32[]{:S(2)}, u32[]{:S(2)}) async-start(bf16[32,8,1024]{2,0,1:T(8,128)(2,1)} %bitcast.97), calls=%async_computation | async-start | bytes 1048576 | tf_op jit(solution)/shard_map/all_to_all | solution.py:24
  53.3 3.6 %collective-permute-start.6 = (bf16[256,128]{1,0:T(8,128)(2,1)S(1)}, bf16[256,128]{1,0:T(8,128)(2,1)S(1)}, u32[]{:S(2)}, u32[]{:S(2)}) collective-permute-start(bf16[256,128]{1,0:T(8,128)(2,1)S(1)} %bitcast.146), channel_id=1, source_target_pairs={{0,48},{8,56},{16,64},{24,72},{32,80},{40,88},{48,96},{56,104},{64... | collective-permute-start | bytes 196616 | tf_op jit(solution)/shard_map/ppermute | solution.py:14
  57.5 5.7 %collective-permute-start.7 = (bf16[256,128]{1,0:T(8,128)(2,1)S(1)}, bf16[256,128]{1,0:T(8,128)(2,1)S(1)}, u32[]{:S(2)}, u32[]{:S(2)}) collective-permute-start(bf16[256,128]{1,0:T(8,128)(2,1)S(1)} %bitcast.147), channel_id=1, source_target_pairs={{0,40},{8,48},{16,56},{24,64},{32,72},{40,80},{48,88},{56,96},{64,... | collective-permute-start | bytes 196616 | tf_op jit(solution)/shard_map/ppermute | solution.py:14
  63.8 2.9 %collective-permute-start.8 = (bf16[256,128]{1,0:T(8,128)(2,1)S(1)}, bf16[256,128]{1,0:T(8,128)(2,1)S(1)}, u32[]{:S(2)}, u32[]{:S(2)}) collective-permute-start(bf16[256,128]{1,0:T(8,128)(2,1)S(1)} %bitcast.148), channel_id=1, source_target_pairs={{0,32},{8,40},{16,48},{24,56},{32,64},{40,72},{48,80},{56,88},{64,... | collective-permute-start | bytes 196616 | tf_op jit(solution)/shard_map/ppermute | solution.py:14
  67.4 1.9 collective-permute-start.9
  69.9 5.0 %collective-permute-start.10 = (bf16[256,128]{1,0:T(8,128)(2,1)S(1)}, bf16[256,128]{1,0:T(8,128)(2,1)S(1)}, u32[]{:S(2)}, u32[]{:S(2)}) collective-permute-start(bf16[256,128]{1,0:T(8,128)(2,1)S(1)} %bitcast.150), channel_id=1, source_target_pairs={{0,16},{8,24},{16,32},{24,40},{32,48},{40,56},{48,64},{56,72},{64,... | collective-permute-start | bytes 196616 | tf_op jit(solution)/shard_map/ppermute | solution.py:14
  76.2 1.9 collective-permute-start.11
  78.2 4.8 %all-to-all-start.2 = ((bf16[32,8,1024]{2,0,1:T(8,128)(2,1)}), bf16[32,8,1024]{2,0,1:T(8,128)(2,1)S(1)}, u32[]{:S(2)}, u32[]{:S(2)}) async-start(bf16[32,8,1024]{2,0,1:T(8,128)(2,1)} %bitcast.96), calls=%async_computation.2 | async-start | bytes 1048576 | tf_op jit(solution)/shard_map/all_to_all | solution.py:27
  84.1 9.2 %all-to-all-done.2 = bf16[32,8,1024]{2,0,1:T(8,128)(2,1)S(1)} async-done(((bf16[32,8,1024]{2,0,1:T(8,128)(2,1)}), bf16[32,8,1024]{2,0,1:T(8,128)(2,1)S(1)}, u32[]{:S(2)}, u32[]{:S(2)}) %all-to-all-start.2) | async-done | bytes 524320 | tf_op jit(solution)/shard_map/all_to_all | solution.py:27
  93.5 78.0 %while.17 = (s32[]{:T(128)}, f32[1792,128]{1,0:T(8,128)}, f32[1792,128]{1,0:T(8,128)}, bf16[4,512,128]{2,1,0:T(8,128)(2,1)}, bf16[4,512,128]{2,1,0:T(8,128)(2,1)...) while((s32[]{:T(128)}, f32[1792,128]{1,0:T(8,128)}, ...), condition=%wide.region_7.8_spmd.clone, body=%wide.region_3.7_spmd.clone.sunk | while | flops 1420753920 | bytes 49303764 | solution.py:84
  93.5 2.2 fusion.54
  96.4 2.7 %fusion.55 = (bf16[512,1792]{1,0:T(8,128)(2,1)S(1)}, f32[512,1792]{1,0:T(8,128)}) fusion(f32[512,1792]{1,0:T(8,128)S(1)} %get-tuple-element.264, f32[512]{0:T(512)S(1)} %log_add_fusion.2, pred[256,1792]{1,0:T(8,128)(4,1)S(1)} %get-tuple-element.303), kind=kLoop, calls=%fused_computation.5.clone.1 | loop fusion | flops 2752512 | bytes 9635840 | tf_op jit(solution)/shard_map/while/body/eval_jaxpr/convert_element_type | solution.py:69
  99.9 4.0 %multiply_convert_fusion.3 = bf16[512,1792]{1,0:T(8,128)(2,1)} fusion(f32[512,1792]{1,0:T(8,128)} %get-tuple-element.266, bf16[1792,128]{1,0:T(8,128)(2,1)S(1)} %get-tuple-element.302, f32[512]{0:T(512)S(1)} %get-tuple-element.268, bf16[1,512,128]{2,1,0:T(8,128)(2,1)S(1)} %constant_dynamic-slice_fusion.2), kind=kOutput, calls=%fused_computation.3.clone.1 | convolution fusion | flops 237633536 | bytes 6096896 | tf_op jit(solution)/shard_map/while/body/eval_jaxpr/dot_general | solution.py:74
  103.9 3.3 %convolution_add_fusion.4 = f32[1792,128]{1,0:T(8,128)} fusion(bf16[512,1792]{1,0:T(8,128)(2,1)} %multiply_convert_fusion.3, f32[1792,128]{1,0:T(8,128)} %get-tuple-element.283, pred[]{:T(512)S(6)} %compare.3, bf16[4,512,128]{2,1,0:T(8,128)(2,1)} %get-tuple-element.299, s32[]{:T(128)} %get-tuple-element.282), kind=kOutput, calls=%fused_computation.7.clone.1 | convolution fusion | flops 235339776 | bytes 3801601 | tf_op jit(solution)/shard_map/while/body/eval_jaxpr/dot_general | solution.py:79
  107.2 2.3 fusion.56
  111.9 2.2 fusion.54
  114.7 2.7 %fusion.55 = (bf16[512,1792]{1,0:T(8,128)(2,1)S(1)}, f32[512,1792]{1,0:T(8,128)}) fusion(f32[512,1792]{1,0:T(8,128)S(1)} %get-tuple-element.264, f32[512]{0:T(512)S(1)} %log_add_fusion.2, pred[256,1792]{1,0:T(8,128)(4,1)S(1)} %get-tuple-element.303), kind=kLoop, calls=%fused_computation.5.clone.1 | loop fusion | flops 2752512 | bytes 9635840 | tf_op jit(solution)/shard_map/while/body/eval_jaxpr/convert_element_type | solution.py:69
  118.3 3.9 %multiply_convert_fusion.3 = bf16[512,1792]{1,0:T(8,128)(2,1)} fusion(f32[512,1792]{1,0:T(8,128)} %get-tuple-element.266, bf16[1792,128]{1,0:T(8,128)(2,1)S(1)} %get-tuple-element.302, f32[512]{0:T(512)S(1)} %get-tuple-element.268, bf16[1,512,128]{2,1,0:T(8,128)(2,1)S(1)} %constant_dynamic-slice_fusion.2), kind=kOutput, calls=%fused_computation.3.clone.1 | convolution fusion | flops 237633536 | bytes 6096896 | tf_op jit(solution)/shard_map/while/body/eval_jaxpr/dot_general | solution.py:74
  122.3 3.5 %convolution_add_fusion.4 = f32[1792,128]{1,0:T(8,128)} fusion(bf16[512,1792]{1,0:T(8,128)(2,1)} %multiply_convert_fusion.3, f32[1792,128]{1,0:T(8,128)} %get-tuple-element.283, pred[]{:T(512)S(6)} %compare.3, bf16[4,512,128]{2,1,0:T(8,128)(2,1)} %get-tuple-element.299, s32[]{:T(128)} %get-tuple-element.282), kind=kOutput, calls=%fused_computation.7.clone.1 | convolution fusion | flops 235339776 | bytes 3801601 | tf_op jit(solution)/shard_map/while/body/eval_jaxpr/dot_general | solution.py:79
  125.8 2.3 fusion.56
  128.9 2.8 %convolution_add_fusion.5 = f32[1792,128]{1,0:T(8,128)} fusion(bf16[512,1792]{1,0:T(8,128)(2,1)S(1)} %get-tuple-element.267, f32[1792,128]{1,0:T(8,128)} %get-tuple-element.284, pred[]{:T(512)S(6)} %compare.3, bf16[1,512,128]{2,1,0:T(8,128)(2,1)S(1)} %constant_dynamic-slice_fusion.2), kind=kOutput, calls=%fused_computation.6.clone.1 | convolution fusion | flops 235339776 | bytes 3801089 | tf_op jit(solution)/shard_map/while/body/eval_jaxpr/dot_general | solution.py:80
  131.8 2.2 fusion.54
  134.6 2.7 %fusion.55 = (bf16[512,1792]{1,0:T(8,128)(2,1)S(1)}, f32[512,1792]{1,0:T(8,128)}) fusion(f32[512,1792]{1,0:T(8,128)S(1)} %get-tuple-element.264, f32[512]{0:T(512)S(1)} %log_add_fusion.2, pred[256,1792]{1,0:T(8,128)(4,1)S(1)} %get-tuple-element.303), kind=kLoop, calls=%fused_computation.5.clone.1 | loop fusion | flops 2752512 | bytes 9635840 | tf_op jit(solution)/shard_map/while/body/eval_jaxpr/convert_element_type | solution.py:69
  138.2 4.0 %multiply_convert_fusion.3 = bf16[512,1792]{1,0:T(8,128)(2,1)} fusion(f32[512,1792]{1,0:T(8,128)} %get-tuple-element.266, bf16[1792,128]{1,0:T(8,128)(2,1)S(1)} %get-tuple-element.302, f32[512]{0:T(512)S(1)} %get-tuple-element.268, bf16[1,512,128]{2,1,0:T(8,128)(2,1)S(1)} %constant_dynamic-slice_fusion.2), kind=kOutput, calls=%fused_computation.3.clone.1 | convolution fusion | flops 237633536 | bytes 6096896 | tf_op jit(solution)/shard_map/while/body/eval_jaxpr/dot_general | solution.py:74
  142.1 3.5 %convolution_add_fusion.4 = f32[1792,128]{1,0:T(8,128)} fusion(bf16[512,1792]{1,0:T(8,128)(2,1)} %multiply_convert_fusion.3, f32[1792,128]{1,0:T(8,128)} %get-tuple-element.283, pred[]{:T(512)S(6)} %compare.3, bf16[4,512,128]{2,1,0:T(8,128)(2,1)} %get-tuple-element.299, s32[]{:T(128)} %get-tuple-element.282), kind=kOutput, calls=%fused_computation.7.clone.1 | convolution fusion | flops 235339776 | bytes 3801601 | tf_op jit(solution)/shard_map/while/body/eval_jaxpr/dot_general | solution.py:79
  145.7 2.3 fusion.56
  148.8 2.8 %convolution_add_fusion.5 = f32[1792,128]{1,0:T(8,128)} fusion(bf16[512,1792]{1,0:T(8,128)(2,1)S(1)} %get-tuple-element.267, f32[1792,128]{1,0:T(8,128)} %get-tuple-element.284, pred[]{:T(512)S(6)} %compare.3, bf16[1,512,128]{2,1,0:T(8,128)(2,1)S(1)} %constant_dynamic-slice_fusion.2), kind=kOutput, calls=%fused_computation.6.clone.1 | convolution fusion | flops 235339776 | bytes 3801089 | tf_op jit(solution)/shard_map/while/body/eval_jaxpr/dot_general | solution.py:80
  151.6 2.2 fusion.54
  154.5 2.7 %fusion.55 = (bf16[512,1792]{1,0:T(8,128)(2,1)S(1)}, f32[512,1792]{1,0:T(8,128)}) fusion(f32[512,1792]{1,0:T(8,128)S(1)} %get-tuple-element.264, f32[512]{0:T(512)S(1)} %log_add_fusion.2, pred[256,1792]{1,0:T(8,128)(4,1)S(1)} %get-tuple-element.303), kind=kLoop, calls=%fused_computation.5.clone.1 | loop fusion | flops 2752512 | bytes 9635840 | tf_op jit(solution)/shard_map/while/body/eval_jaxpr/convert_element_type | solution.py:69
  158.1 3.9 %multiply_convert_fusion.3 = bf16[512,1792]{1,0:T(8,128)(2,1)} fusion(f32[512,1792]{1,0:T(8,128)} %get-tuple-element.266, bf16[1792,128]{1,0:T(8,128)(2,1)S(1)} %get-tuple-element.302, f32[512]{0:T(512)S(1)} %get-tuple-element.268, bf16[1,512,128]{2,1,0:T(8,128)(2,1)S(1)} %constant_dynamic-slice_fusion.2), kind=kOutput, calls=%fused_computation.3.clone.1 | convolution fusion | flops 237633536 | bytes 6096896 | tf_op jit(solution)/shard_map/while/body/eval_jaxpr/dot_general | solution.py:74
  162.0 3.5 %convolution_add_fusion.4 = f32[1792,128]{1,0:T(8,128)} fusion(bf16[512,1792]{1,0:T(8,128)(2,1)} %multiply_convert_fusion.3, f32[1792,128]{1,0:T(8,128)} %get-tuple-element.283, pred[]{:T(512)S(6)} %compare.3, bf16[4,512,128]{2,1,0:T(8,128)(2,1)} %get-tuple-element.299, s32[]{:T(128)} %get-tuple-element.282), kind=kOutput, calls=%fused_computation.7.clone.1 | convolution fusion | flops 235339776 | bytes 3801601 | tf_op jit(solution)/shard_map/while/body/eval_jaxpr/dot_general | solution.py:79
  165.5 2.3 fusion.56
  168.7 2.8 %convolution_add_fusion.5 = f32[1792,128]{1,0:T(8,128)} fusion(bf16[512,1792]{1,0:T(8,128)(2,1)S(1)} %get-tuple-element.267, f32[1792,128]{1,0:T(8,128)} %get-tuple-element.284, pred[]{:T(512)S(6)} %compare.3, bf16[1,512,128]{2,1,0:T(8,128)(2,1)S(1)} %constant_dynamic-slice_fusion.2), kind=kOutput, calls=%fused_computation.6.clone.1 | convolution fusion | flops 235339776 | bytes 3801089 | tf_op jit(solution)/shard_map/while/body/eval_jaxpr/dot_general | solution.py:80
  172.8 4.1 %collective-permute-start.18 = (f32[256,128]{1,0:T(8,128)S(1)}, f32[256,128]{1,0:T(8,128)S(1)}, u32[]{:S(2)}, u32[]{:S(2)}) collective-permute-start(f32[256,128]{1,0:T(8,128)S(1)} %get-tuple-element.185), channel_id=1, source_target_pairs={{8,0},{16,8},{24,16},{32,24},{40,32},{48,40},{56,48},{64,56},{72,6... | collective-permute-start | bytes 393224 | tf_op jit(solution)/shard_map/ppermute | solution.py:14
  176.9 4.4 %collective-permute-start.19 = (f32[256,128]{1,0:T(8,128)S(1)}, f32[256,128]{1,0:T(8,128)S(1)}, u32[]{:S(2)}, u32[]{:S(2)}) collective-permute-start(f32[256,128]{1,0:T(8,128)S(1)} %get-tuple-element.188), channel_id=1, source_target_pairs={{16,0},{24,8},{32,16},{40,24},{48,32},{56,40},{64,48},{72,56},{80,... | collective-permute-start | bytes 393224 | tf_op jit(solution)/shard_map/ppermute | solution.py:14
  181.3 2.7 %collective-permute-start.20 = (f32[256,128]{1,0:T(8,128)S(1)}, f32[256,128]{1,0:T(8,128)S(1)}, u32[]{:S(2)}, u32[]{:S(2)}) collective-permute-start(f32[256,128]{1,0:T(8,128)S(1)} %get-tuple-element.187), channel_id=1, source_target_pairs={{24,0},{32,8},{40,16},{48,24},{56,32},{64,40},{72,48},{80,56},{88,... | collective-permute-start | bytes 393224 | tf_op jit(solution)/shard_map/ppermute | solution.py:14
  184.0 2.9 %collective-permute-start.21 = (f32[256,128]{1,0:T(8,128)S(1)}, f32[256,128]{1,0:T(8,128)S(1)}, u32[]{:S(2)}, u32[]{:S(2)}) collective-permute-start(f32[256,128]{1,0:T(8,128)S(1)} %get-tuple-element.186), channel_id=1, source_target_pairs={{32,0},{40,8},{48,16},{56,24},{64,32},{72,40},{80,48},{88,56},{96,... | collective-permute-start | bytes 393224 | tf_op jit(solution)/shard_map/ppermute | solution.py:14
  187.0 3.0 %collective-permute-start.22 = (f32[256,128]{1,0:T(8,128)S(1)}, f32[256,128]{1,0:T(8,128)S(1)}, u32[]{:S(2)}, u32[]{:S(2)}) collective-permute-start(f32[256,128]{1,0:T(8,128)S(1)} %get-tuple-element.190), channel_id=1, source_target_pairs={{40,0},{48,8},{56,16},{64,24},{72,32},{80,40},{88,48},{96,56},{104... | collective-permute-start | bytes 393224 | tf_op jit(solution)/shard_map/ppermute | solution.py:14
  191.3 2.1 collective-permute-start.23
  193.4 3.8 %collective-permute-start.12 = (f32[256,128]{1,0:T(8,128)S(1)}, f32[256,128]{1,0:T(8,128)S(1)}, u32[]{:S(2)}, u32[]{:S(2)}) collective-permute-start(f32[256,128]{1,0:T(8,128)S(1)} %get-tuple-element.191), channel_id=1, source_target_pairs={{8,0},{16,8},{24,16},{32,24},{40,32},{48,40},{56,48},{64,56},{72,6... | collective-permute-start | bytes 393224 | tf_op jit(solution)/shard_map/ppermute | solution.py:14
  197.2 3.1 %collective-permute-start.13 = (f32[256,128]{1,0:T(8,128)S(1)}, f32[256,128]{1,0:T(8,128)S(1)}, u32[]{:S(2)}, u32[]{:S(2)}) collective-permute-start(f32[256,128]{1,0:T(8,128)S(1)} %get-tuple-element.194), channel_id=1, source_target_pairs={{16,0},{24,8},{32,16},{40,24},{48,32},{56,40},{64,48},{72,56},{80,... | collective-permute-start | bytes 393224 | tf_op jit(solution)/shard_map/ppermute | solution.py:14
  200.3 1.9 collective-permute-start.14
  202.2 1.9 collective-permute-start.15
  204.2 2.1 collective-permute-done.23
  206.2 1.9 collective-permute-start.16
  208.2 3.1 %collective-permute-start.17 = (f32[256,128]{1,0:T(8,128)S(1)}, f32[256,128]{1,0:T(8,128)S(1)}, u32[]{:S(2)}, u32[]{:S(2)}) collective-permute-start(f32[256,128]{1,0:T(8,128)S(1)} %get-tuple-element.195), channel_id=1, source_target_pairs={{48,0},{56,8},{64,16},{72,24},{80,32},{88,40},{96,48},{104,56},{11... | collective-permute-start | bytes 393224 | tf_op jit(solution)/shard_map/ppermute | solution.py:14
  212.9 3.4 %all-to-all-start.7 = ((bf16[8,32,128]{2,1,0:T(8,128)(2,1)}), bf16[8,32,128]{2,1,0:T(8,128)(2,1)S(1)}, u32[]{:S(2)}, u32[]{:S(2)}) async-start(bf16[8,32,128]{2,1,0:T(8,128)(2,1)} %bitcast.21), calls=%async_computation.7 | async-start | bytes 131072 | tf_op jit(solution)/shard_map/all_to_all | solution.py:109
  216.6 12.9 %collective-permute-done.17 = f32[256,128]{1,0:T(8,128)S(1)} collective-permute-done((f32[256,128]{1,0:T(8,128)S(1)}, f32[256,128]{1,0:T(8,128)S(1)}, u32[]{:S(2)}, u32[]{:S(2)}) %collective-permute-start.17) | collective-permute-done | bytes 131104 | tf_op jit(solution)/shard_map/ppermute | solution.py:14
  231.1 3.4 %all-to-all-start.6 = ((bf16[8,32,128]{2,1,0:T(8,128)(2,1)}), bf16[8,32,128]{2,1,0:T(8,128)(2,1)S(1)}, u32[]{:S(2)}, u32[]{:S(2)}) async-start(bf16[8,32,128]{2,1,0:T(8,128)(2,1)} %bitcast.19), calls=%async_computation.6 | async-start | bytes 131072 | tf_op jit(solution)/shard_map/all_to_all | solution.py:108
  235.8 4.2 %all-to-all-done.6 = bf16[8,32,128]{2,1,0:T(8,128)(2,1)S(1)} async-done(((bf16[8,32,128]{2,1,0:T(8,128)(2,1)}), bf16[8,32,128]{2,1,0:T(8,128)(2,1)S(1)}, u32[]{:S(2)}, u32[]{:S(2)}) %all-to-all-start.6) | async-done | bytes 65568 | tf_op jit(solution)/shard_map/all_to_all | solution.py:108
  240.0 3.5 %all-to-all-start.4 = ((bf16[8,32,1024]{2,1,0:T(8,128)(2,1)}), bf16[8,32,1024]{2,1,0:T(8,128)(2,1)S(1)}, u32[]{:S(2)}, u32[]{:S(2)}) async-start(bf16[8,32,1024]{2,1,0:T(8,128)(2,1)} %all_to_all.122), calls=%async_computation.4 | async-start | bytes 1048576 | tf_op jit(solution)/shard_map/all_to_all | solution.py:106
  244.9 8.9 %all-to-all-done.4 = bf16[8,32,1024]{2,1,0:T(8,128)(2,1)S(1)} async-done(((bf16[8,32,1024]{2,1,0:T(8,128)(2,1)}), bf16[8,32,1024]{2,1,0:T(8,128)(2,1)S(1)}, u32[]{:S(2)}, u32[]{:S(2)}) %all-to-all-start.4) | async-done | bytes 524320 | tf_op jit(solution)/shard_map/all_to_all | solution.py:106
  253.8 3.5 %all-to-all-start.5 = ((bf16[8,32,1024]{2,1,0:T(8,128)(2,1)}), bf16[8,32,1024]{2,1,0:T(8,128)(2,1)S(1)}, u32[]{:S(2)}, u32[]{:S(2)}) async-start(bf16[8,32,1024]{2,1,0:T(8,128)(2,1)} %all_to_all.126), calls=%async_computation.5 | async-start | bytes 1048576 | tf_op jit(solution)/shard_map/all_to_all | solution.py:107
  259.4 8.2 %all-to-all-done.5 = bf16[8,32,1024]{2,1,0:T(8,128)(2,1)S(1)} async-done(((bf16[8,32,1024]{2,1,0:T(8,128)(2,1)}), bf16[8,32,1024]{2,1,0:T(8,128)(2,1)S(1)}, u32[]{:S(2)}, u32[]{:S(2)}) %all-to-all-start.5) | async-done | bytes 524320 | tf_op jit(solution)/shard_map/all_to_all | solution.py:107
  (132 shorter events, 34.9 us)
Async XLA Ops:
  0.6 0.8 copy-start
  2.1 10.1 %all-to-all-start.1 = ((bf16[32,8,128]{2,0,1:T(8,128)(2,1)}), bf16[32,8,128]{2,0,1:T(8,128)(2,1)S(1)}, u32[]{:S(2)}, u32[]{:S(2)}) async-start(bf16[32,8,128]{2,0,1:T(8,128)(2,1)} %copy_bitcast_fusion.6), calls=%async_computation.1 | async-start | bytes 131072 | tf_op jit(solution)/shard_map/all_to_all | solution.py:25
  12.2 36.4 %all-to-all-start.3 = ((bf16[32,8,128]{2,0,1:T(8,128)(2,1)}), bf16[32,8,128]{2,0,1:T(8,128)(2,1)S(1)}, u32[]{:S(2)}, u32[]{:S(2)}) async-start(bf16[32,8,128]{2,0,1:T(8,128)(2,1)} %copy_bitcast_fusion.5), calls=%async_computation.3 | async-start | bytes 131072 | tf_op jit(solution)/shard_map/all_to_all | solution.py:26
  15.6 30.5 %collective-permute-start = (bf16[256,128]{1,0:T(8,128)(2,1)S(1)}, bf16[256,128]{1,0:T(8,128)(2,1)S(1)}, u32[]{:S(2)}, u32[]{:S(2)}) collective-permute-start(bf16[256,128]{1,0:T(8,128)(2,1)S(1)} %bitcast.153), channel_id=1, source_target_pairs={{0,48},{8,56},{16,64},{24,72},{32,80},{40,88},{48,96},{56,104},{64... | collective-permute-start | bytes 196616 | tf_op jit(solution)/shard_map/ppermute | solution.py:14
  26.3 27.0 %collective-permute-start.1 = (bf16[256,128]{1,0:T(8,128)(2,1)S(1)}, bf16[256,128]{1,0:T(8,128)(2,1)S(1)}, u32[]{:S(2)}, u32[]{:S(2)}) collective-permute-start(bf16[256,128]{1,0:T(8,128)(2,1)S(1)} %bitcast.154), channel_id=1, source_target_pairs={{0,40},{8,48},{16,56},{24,64},{32,72},{40,80},{48,88},{56,96},{64,... | collective-permute-start | bytes 196616 | tf_op jit(solution)/shard_map/ppermute | solution.py:14
  31.6 25.9 %collective-permute-start.2 = (bf16[256,128]{1,0:T(8,128)(2,1)S(1)}, bf16[256,128]{1,0:T(8,128)(2,1)S(1)}, u32[]{:S(2)}, u32[]{:S(2)}) collective-permute-start(bf16[256,128]{1,0:T(8,128)(2,1)S(1)} %bitcast.155), channel_id=1, source_target_pairs={{0,32},{8,40},{16,48},{24,56},{32,64},{40,72},{48,80},{56,88},{64,... | collective-permute-start | bytes 196616 | tf_op jit(solution)/shard_map/ppermute | solution.py:14
  35.5 28.3 %collective-permute-start.3 = (bf16[256,128]{1,0:T(8,128)(2,1)S(1)}, bf16[256,128]{1,0:T(8,128)(2,1)S(1)}, u32[]{:S(2)}, u32[]{:S(2)}) collective-permute-start(bf16[256,128]{1,0:T(8,128)(2,1)S(1)} %bitcast.156), channel_id=1, source_target_pairs={{0,24},{8,32},{16,40},{24,48},{32,56},{40,64},{48,72},{56,80},{64,... | collective-permute-start | bytes 196616 | tf_op jit(solution)/shard_map/ppermute | solution.py:14
  39.9 27.5 %collective-permute-start.4 = (bf16[256,128]{1,0:T(8,128)(2,1)S(1)}, bf16[256,128]{1,0:T(8,128)(2,1)S(1)}, u32[]{:S(2)}, u32[]{:S(2)}) collective-permute-start(bf16[256,128]{1,0:T(8,128)(2,1)S(1)} %bitcast.157), channel_id=1, source_target_pairs={{0,16},{8,24},{16,32},{24,40},{32,48},{40,56},{48,64},{56,72},{64,... | collective-permute-start | bytes 196616 | tf_op jit(solution)/shard_map/ppermute | solution.py:14
  46.1 23.9 %collective-permute-start.5 = (bf16[256,128]{1,0:T(8,128)(2,1)S(1)}, bf16[256,128]{1,0:T(8,128)(2,1)S(1)}, u32[]{:S(2)}, u32[]{:S(2)}) collective-permute-start(bf16[256,128]{1,0:T(8,128)(2,1)S(1)} %bitcast.158), channel_id=1, source_target_pairs={{0,8},{8,16},{16,24},{24,32},{32,40},{40,48},{48,56},{56,64},{64,7... | collective-permute-start | bytes 196616 | tf_op jit(solution)/shard_map/ppermute | solution.py:14
  48.6 29.5 %all-to-all-start = ((bf16[32,8,1024]{2,0,1:T(8,128)(2,1)}), bf16[32,8,1024]{2,0,1:T(8,128)(2,1)S(1)}, u32[]{:S(2)}, u32[]{:S(2)}) async-start(bf16[32,8,1024]{2,0,1:T(8,128)(2,1)} %bitcast.97), calls=%async_computation | async-start | bytes 1048576 | tf_op jit(solution)/shard_map/all_to_all | solution.py:24
  53.3 22.9 %collective-permute-start.6 = (bf16[256,128]{1,0:T(8,128)(2,1)S(1)}, bf16[256,128]{1,0:T(8,128)(2,1)S(1)}, u32[]{:S(2)}, u32[]{:S(2)}) collective-permute-start(bf16[256,128]{1,0:T(8,128)(2,1)S(1)} %bitcast.146), channel_id=1, source_target_pairs={{0,48},{8,56},{16,64},{24,72},{32,80},{40,88},{48,96},{56,104},{64... | collective-permute-start | bytes 196616 | tf_op jit(solution)/shard_map/ppermute | solution.py:14
  57.5 20.6 %collective-permute-start.7 = (bf16[256,128]{1,0:T(8,128)(2,1)S(1)}, bf16[256,128]{1,0:T(8,128)(2,1)S(1)}, u32[]{:S(2)}, u32[]{:S(2)}) collective-permute-start(bf16[256,128]{1,0:T(8,128)(2,1)S(1)} %bitcast.147), channel_id=1, source_target_pairs={{0,40},{8,48},{16,56},{24,64},{32,72},{40,80},{48,88},{56,96},{64,... | collective-permute-start | bytes 196616 | tf_op jit(solution)/shard_map/ppermute | solution.py:14
  63.8 19.2 %collective-permute-start.8 = (bf16[256,128]{1,0:T(8,128)(2,1)S(1)}, bf16[256,128]{1,0:T(8,128)(2,1)S(1)}, u32[]{:S(2)}, u32[]{:S(2)}) collective-permute-start(bf16[256,128]{1,0:T(8,128)(2,1)S(1)} %bitcast.148), channel_id=1, source_target_pairs={{0,32},{8,40},{16,48},{24,56},{32,64},{40,72},{48,80},{56,88},{64,... | collective-permute-start | bytes 196616 | tf_op jit(solution)/shard_map/ppermute | solution.py:14
  67.4 15.6 %collective-permute-start.9 = (bf16[256,128]{1,0:T(8,128)(2,1)S(1)}, bf16[256,128]{1,0:T(8,128)(2,1)S(1)}, u32[]{:S(2)}, u32[]{:S(2)}) collective-permute-start(bf16[256,128]{1,0:T(8,128)(2,1)S(1)} %bitcast.149), channel_id=1, source_target_pairs={{0,24},{8,32},{16,40},{24,48},{32,56},{40,64},{48,72},{56,80},{64,... | collective-permute-start | bytes 196616 | tf_op jit(solution)/shard_map/ppermute | solution.py:14
  69.9 13.1 %collective-permute-start.10 = (bf16[256,128]{1,0:T(8,128)(2,1)S(1)}, bf16[256,128]{1,0:T(8,128)(2,1)S(1)}, u32[]{:S(2)}, u32[]{:S(2)}) collective-permute-start(bf16[256,128]{1,0:T(8,128)(2,1)S(1)} %bitcast.150), channel_id=1, source_target_pairs={{0,16},{8,24},{16,32},{24,40},{32,48},{40,56},{48,64},{56,72},{64,... | collective-permute-start | bytes 196616 | tf_op jit(solution)/shard_map/ppermute | solution.py:14
  76.2 6.9 %collective-permute-start.11 = (bf16[256,128]{1,0:T(8,128)(2,1)S(1)}, bf16[256,128]{1,0:T(8,128)(2,1)S(1)}, u32[]{:S(2)}, u32[]{:S(2)}) collective-permute-start(bf16[256,128]{1,0:T(8,128)(2,1)S(1)} %bitcast.151), channel_id=1, source_target_pairs={{0,8},{8,16},{16,24},{24,32},{32,40},{40,48},{48,56},{56,64},{64,7... | collective-permute-start | bytes 196616 | tf_op jit(solution)/shard_map/ppermute | solution.py:14
  78.2 15.2 %all-to-all-start.2 = ((bf16[32,8,1024]{2,0,1:T(8,128)(2,1)}), bf16[32,8,1024]{2,0,1:T(8,128)(2,1)S(1)}, u32[]{:S(2)}, u32[]{:S(2)}) async-start(bf16[32,8,1024]{2,0,1:T(8,128)(2,1)} %bitcast.96), calls=%async_computation.2 | async-start | bytes 1048576 | tf_op jit(solution)/shard_map/all_to_all | solution.py:27
  93.5 5.5 %copy-start.2 = (bf16[4,512,128]{2,1,0:T(8,128)(2,1)}, bf16[4,512,128]{2,1,0:T(8,128)(2,1)S(1)}, u32[]{:S(2)}) copy-start(bf16[4,512,128]{2,1,0:T(8,128)(2,1)S(1)} %get-tuple-element.301) | copy-start | bytes 1572868 | tf_op jit(solution)/shard_map/while
  103.9 3.3 %copy-start.1 = (bf16[512,1792]{1,0:T(8,128)(2,1)S(1)}, bf16[512,1792]{1,0:T(8,128)(2,1)}, u32[]{:S(2)}) copy-start(bf16[512,1792]{1,0:T(8,128)(2,1)} %multiply_convert_fusion.3) | copy-start | bytes 5505028 | tf_op jit(solution)/shard_map/while
  110.3 1.6 copy-start.3
  111.9 5.5 %copy-start.2 = (bf16[4,512,128]{2,1,0:T(8,128)(2,1)}, bf16[4,512,128]{2,1,0:T(8,128)(2,1)S(1)}, u32[]{:S(2)}) copy-start(bf16[4,512,128]{2,1,0:T(8,128)(2,1)S(1)} %get-tuple-element.301) | copy-start | bytes 1572868 | tf_op jit(solution)/shard_map/while
  122.3 3.5 %copy-start.1 = (bf16[512,1792]{1,0:T(8,128)(2,1)S(1)}, bf16[512,1792]{1,0:T(8,128)(2,1)}, u32[]{:S(2)}) copy-start(bf16[512,1792]{1,0:T(8,128)(2,1)} %multiply_convert_fusion.3) | copy-start | bytes 5505028 | tf_op jit(solution)/shard_map/while
  128.9 2.8 %copy-start.3 = (bf16[4,512,128]{2,1,0:T(8,128)(2,1)S(1)}, bf16[4,512,128]{2,1,0:T(8,128)(2,1)}, u32[]{:S(2)}) copy-start(bf16[4,512,128]{2,1,0:T(8,128)(2,1)} %copy-done.2) | copy-start | bytes 1572868 | tf_op jit(solution)/shard_map/while
  131.8 5.5 %copy-start.2 = (bf16[4,512,128]{2,1,0:T(8,128)(2,1)}, bf16[4,512,128]{2,1,0:T(8,128)(2,1)S(1)}, u32[]{:S(2)}) copy-start(bf16[4,512,128]{2,1,0:T(8,128)(2,1)S(1)} %get-tuple-element.301) | copy-start | bytes 1572868 | tf_op jit(solution)/shard_map/while
  142.1 3.5 %copy-start.1 = (bf16[512,1792]{1,0:T(8,128)(2,1)S(1)}, bf16[512,1792]{1,0:T(8,128)(2,1)}, u32[]{:S(2)}) copy-start(bf16[512,1792]{1,0:T(8,128)(2,1)} %multiply_convert_fusion.3) | copy-start | bytes 5505028 | tf_op jit(solution)/shard_map/while
  148.8 2.8 %copy-start.3 = (bf16[4,512,128]{2,1,0:T(8,128)(2,1)S(1)}, bf16[4,512,128]{2,1,0:T(8,128)(2,1)}, u32[]{:S(2)}) copy-start(bf16[4,512,128]{2,1,0:T(8,128)(2,1)} %copy-done.2) | copy-start | bytes 1572868 | tf_op jit(solution)/shard_map/while
  151.6 5.5 %copy-start.2 = (bf16[4,512,128]{2,1,0:T(8,128)(2,1)}, bf16[4,512,128]{2,1,0:T(8,128)(2,1)S(1)}, u32[]{:S(2)}) copy-start(bf16[4,512,128]{2,1,0:T(8,128)(2,1)S(1)} %get-tuple-element.301) | copy-start | bytes 1572868 | tf_op jit(solution)/shard_map/while
  162.0 3.5 %copy-start.1 = (bf16[512,1792]{1,0:T(8,128)(2,1)S(1)}, bf16[512,1792]{1,0:T(8,128)(2,1)}, u32[]{:S(2)}) copy-start(bf16[512,1792]{1,0:T(8,128)(2,1)} %multiply_convert_fusion.3) | copy-start | bytes 5505028 | tf_op jit(solution)/shard_map/while
  168.7 2.8 %copy-start.3 = (bf16[4,512,128]{2,1,0:T(8,128)(2,1)S(1)}, bf16[4,512,128]{2,1,0:T(8,128)(2,1)}, u32[]{:S(2)}) copy-start(bf16[4,512,128]{2,1,0:T(8,128)(2,1)} %copy-done.2) | copy-start | bytes 1572868 | tf_op jit(solution)/shard_map/while
  171.5 63.0 %copy-start.4 = (bf16[4,512,128]{2,1,0:T(8,128)(2,1)S(1)}, bf16[4,512,128]{2,1,0:T(8,128)(2,1)}, u32[]{:S(2)}) copy-start(bf16[4,512,128]{2,1,0:T(8,128)(2,1)} %get-tuple-element.59) | copy-start | bytes 1572868
  172.8 70.7 %copy-start.5 = (bf16[4,512,128]{2,1,0:T(8,128)(2,1)S(1)}, bf16[4,512,128]{2,1,0:T(8,128)(2,1)}, u32[]{:S(2)}) copy-start(bf16[4,512,128]{2,1,0:T(8,128)(2,1)} %get-tuple-element.60) | copy-start | bytes 1572868
  172.8 18.4 %collective-permute-start.18 = (f32[256,128]{1,0:T(8,128)S(1)}, f32[256,128]{1,0:T(8,128)S(1)}, u32[]{:S(2)}, u32[]{:S(2)}) collective-permute-start(f32[256,128]{1,0:T(8,128)S(1)} %get-tuple-element.185), channel_id=1, source_target_pairs={{8,0},{16,8},{24,16},{32,24},{40,32},{48,40},{56,48},{64,56},{72,6... | collective-permute-start | bytes 393224 | tf_op jit(solution)/shard_map/ppermute | solution.py:14
  176.9 16.5 %collective-permute-start.19 = (f32[256,128]{1,0:T(8,128)S(1)}, f32[256,128]{1,0:T(8,128)S(1)}, u32[]{:S(2)}, u32[]{:S(2)}) collective-permute-start(f32[256,128]{1,0:T(8,128)S(1)} %get-tuple-element.188), channel_id=1, source_target_pairs={{16,0},{24,8},{32,16},{40,24},{48,32},{56,40},{64,48},{72,56},{80,... | collective-permute-start | bytes 393224 | tf_op jit(solution)/shard_map/ppermute | solution.py:14
  181.3 15.9 %collective-permute-start.20 = (f32[256,128]{1,0:T(8,128)S(1)}, f32[256,128]{1,0:T(8,128)S(1)}, u32[]{:S(2)}, u32[]{:S(2)}) collective-permute-start(f32[256,128]{1,0:T(8,128)S(1)} %get-tuple-element.187), channel_id=1, source_target_pairs={{24,0},{32,8},{40,16},{48,24},{56,32},{64,40},{72,48},{80,56},{88,... | collective-permute-start | bytes 393224 | tf_op jit(solution)/shard_map/ppermute | solution.py:14
  184.0 16.3 %collective-permute-start.21 = (f32[256,128]{1,0:T(8,128)S(1)}, f32[256,128]{1,0:T(8,128)S(1)}, u32[]{:S(2)}, u32[]{:S(2)}) collective-permute-start(f32[256,128]{1,0:T(8,128)S(1)} %get-tuple-element.186), channel_id=1, source_target_pairs={{32,0},{40,8},{48,16},{56,24},{64,32},{72,40},{80,48},{88,56},{96,... | collective-permute-start | bytes 393224 | tf_op jit(solution)/shard_map/ppermute | solution.py:14
  187.0 15.3 %collective-permute-start.22 = (f32[256,128]{1,0:T(8,128)S(1)}, f32[256,128]{1,0:T(8,128)S(1)}, u32[]{:S(2)}, u32[]{:S(2)}) collective-permute-start(f32[256,128]{1,0:T(8,128)S(1)} %get-tuple-element.190), channel_id=1, source_target_pairs={{40,0},{48,8},{56,16},{64,24},{72,32},{80,40},{88,48},{96,56},{104... | collective-permute-start | bytes 393224 | tf_op jit(solution)/shard_map/ppermute | solution.py:14
  191.3 15.0 %collective-permute-start.23 = (f32[256,128]{1,0:T(8,128)S(1)}, f32[256,128]{1,0:T(8,128)S(1)}, u32[]{:S(2)}, u32[]{:S(2)}) collective-permute-start(f32[256,128]{1,0:T(8,128)S(1)} %get-tuple-element.189), channel_id=1, source_target_pairs={{48,0},{56,8},{64,16},{72,24},{80,32},{88,40},{96,48},{104,56},{11... | collective-permute-start | bytes 393224 | tf_op jit(solution)/shard_map/ppermute | solution.py:14
  193.4 14.8 %collective-permute-start.12 = (f32[256,128]{1,0:T(8,128)S(1)}, f32[256,128]{1,0:T(8,128)S(1)}, u32[]{:S(2)}, u32[]{:S(2)}) collective-permute-start(f32[256,128]{1,0:T(8,128)S(1)} %get-tuple-element.191), channel_id=1, source_target_pairs={{8,0},{16,8},{24,16},{32,24},{40,32},{48,40},{56,48},{64,56},{72,6... | collective-permute-start | bytes 393224 | tf_op jit(solution)/shard_map/ppermute | solution.py:14
  197.2 19.1 %collective-permute-start.13 = (f32[256,128]{1,0:T(8,128)S(1)}, f32[256,128]{1,0:T(8,128)S(1)}, u32[]{:S(2)}, u32[]{:S(2)}) collective-permute-start(f32[256,128]{1,0:T(8,128)S(1)} %get-tuple-element.194), channel_id=1, source_target_pairs={{16,0},{24,8},{32,16},{40,24},{48,32},{56,40},{64,48},{72,56},{80,... | collective-permute-start | bytes 393224 | tf_op jit(solution)/shard_map/ppermute | solution.py:14
  200.3 16.0 %collective-permute-start.14 = (f32[256,128]{1,0:T(8,128)S(1)}, f32[256,128]{1,0:T(8,128)S(1)}, u32[]{:S(2)}, u32[]{:S(2)}) collective-permute-start(f32[256,128]{1,0:T(8,128)S(1)} %get-tuple-element.193), channel_id=1, source_target_pairs={{24,0},{32,8},{40,16},{48,24},{56,32},{64,40},{72,48},{80,56},{88,... | collective-permute-start | bytes 393224 | tf_op jit(solution)/shard_map/ppermute | solution.py:14
  202.2 14.1 %collective-permute-start.15 = (f32[256,128]{1,0:T(8,128)S(1)}, f32[256,128]{1,0:T(8,128)S(1)}, u32[]{:S(2)}, u32[]{:S(2)}) collective-permute-start(f32[256,128]{1,0:T(8,128)S(1)} %get-tuple-element.192), channel_id=1, source_target_pairs={{32,0},{40,8},{48,16},{56,24},{64,32},{72,40},{80,48},{88,56},{96,... | collective-permute-start | bytes 393224 | tf_op jit(solution)/shard_map/ppermute | solution.py:14
  206.2 10.4 %collective-permute-start.16 = (f32[256,128]{1,0:T(8,128)S(1)}, f32[256,128]{1,0:T(8,128)S(1)}, u32[]{:S(2)}, u32[]{:S(2)}) collective-permute-start(f32[256,128]{1,0:T(8,128)S(1)} %get-tuple-element.196), channel_id=1, source_target_pairs={{40,0},{48,8},{56,16},{64,24},{72,32},{80,40},{88,48},{96,56},{104... | collective-permute-start | bytes 393224 | tf_op jit(solution)/shard_map/ppermute | solution.py:14
  208.2 21.3 %collective-permute-start.17 = (f32[256,128]{1,0:T(8,128)S(1)}, f32[256,128]{1,0:T(8,128)S(1)}, u32[]{:S(2)}, u32[]{:S(2)}) collective-permute-start(f32[256,128]{1,0:T(8,128)S(1)} %get-tuple-element.195), channel_id=1, source_target_pairs={{48,0},{56,8},{64,16},{72,24},{80,32},{88,40},{96,48},{104,56},{11... | collective-permute-start | bytes 393224 | tf_op jit(solution)/shard_map/ppermute | solution.py:14
  212.9 18.2 %all-to-all-start.7 = ((bf16[8,32,128]{2,1,0:T(8,128)(2,1)}), bf16[8,32,128]{2,1,0:T(8,128)(2,1)S(1)}, u32[]{:S(2)}, u32[]{:S(2)}) async-start(bf16[8,32,128]{2,1,0:T(8,128)(2,1)} %bitcast.21), calls=%async_computation.7 | async-start | bytes 131072 | tf_op jit(solution)/shard_map/all_to_all | solution.py:109
  231.1 8.9 %all-to-all-start.6 = ((bf16[8,32,128]{2,1,0:T(8,128)(2,1)}), bf16[8,32,128]{2,1,0:T(8,128)(2,1)S(1)}, u32[]{:S(2)}, u32[]{:S(2)}) async-start(bf16[8,32,128]{2,1,0:T(8,128)(2,1)} %bitcast.19), calls=%async_computation.6 | async-start | bytes 131072 | tf_op jit(solution)/shard_map/all_to_all | solution.py:108
  240.0 13.8 %all-to-all-start.4 = ((bf16[8,32,1024]{2,1,0:T(8,128)(2,1)}), bf16[8,32,1024]{2,1,0:T(8,128)(2,1)S(1)}, u32[]{:S(2)}, u32[]{:S(2)}) async-start(bf16[8,32,1024]{2,1,0:T(8,128)(2,1)} %all_to_all.122), calls=%async_computation.4 | async-start | bytes 1048576 | tf_op jit(solution)/shard_map/all_to_all | solution.py:106
  253.8 13.8 %all-to-all-start.5 = ((bf16[8,32,1024]{2,1,0:T(8,128)(2,1)}), bf16[8,32,1024]{2,1,0:T(8,128)(2,1)S(1)}, u32[]{:S(2)}, u32[]{:S(2)}) async-start(bf16[8,32,1024]{2,1,0:T(8,128)(2,1)} %all_to_all.126), calls=%async_computation.5 | async-start | bytes 1048576 | tf_op jit(solution)/shard_map/all_to_all | solution.py:107
where the time goes:
time: 271 us; the launch traced here: 268 us
  starting transfers between devices  115 us (42%)
  matrix products  60.8 us (22%)
  waiting for transfers between devices  48.8 us (18%)
  local copies, waits for them, and re-layouts  25 us (9%)
  other arithmetic  17.5 us (6%)
    ppermute x24, starting transfers between devices, from_behind(): return lax.ppermute(value, axis, pairs)  84 us
    dot_general x4, matrix products, pair_step(): jnp.dot(grad_rows, val_win.T, preferred_element_type=jnp.float32)  15.8 us
    ppermute x24, waiting for transfers between devices, from_behind(): return lax.ppermute(value, axis, pairs)  15.4 us
    dot_general x4, matrix products, pair_step(): jnp.dot(grad_low.T, query_rows, preferred_element_type=jnp.float32)  13.9 us
    convert_element_type x4, other arithmetic, pair_step(): weights_low = weights.astype(jnp.bfloat16)  10.8 us
    dot_general x4, matrix products, pair_step(): jnp.dot(weights_low.T, grad_rows, preferred_element_type=jnp.float32)  10.1 us
    dot_general x4, matrix products, pair_step(): jnp.dot(grad_low, key_win, preferred_element_type=jnp.float32)  9.26 us
    all_to_all x1, waiting for transfers between devices, body(): lax.all_to_all(grad_out, 'kv', split_axis=1, concat_axis=0, tiled=True)  9.22 us
  transfers between devices with their start and end apart: 32, of which 8 were waited for; matrix products, arithmetic and copies ran while one was open for 7% of the time, Pallas kernels for 0%

commit v1 on v0

v1 whole, which is shorter than its diff:
```python
import functools

import jax
import jax.numpy as jnp
from jax import lax
from jax.experimental import pallas as pl
from jax.experimental.pallas import tpu as pltpu
from jax.sharding import PartitionSpec as P

HD = 128
GROUP = 8
WIN = 6
MESH = pl.DeviceIdType.MESH
SCALE = HD ** (-0.5)
SCALE2 = SCALE * 1.4426950408889634
MASKED = -1e30
F32 = jnp.float32
BF16 = jnp.bfloat16


def any_spec():
    return pl.BlockSpec(memory_space=pl.ANY)


def vmem_spec():
    return pl.BlockSpec(memory_space=pltpu.VMEM)


def remote(src, dst, send, recv, peer):
    return pltpu.make_async_remote_copy(
        src_ref=src, dst_ref=dst, send_sem=send, recv_sem=recv, device_id=peer, device_id_type=MESH
    )


def gather_kernel(nk, ns, q_ref, k_ref, v_ref, g_ref, q_out, g_out, kw, vw, own_sem, send_kv, recv_kv, send_win, recv_win):
    me = lax.axis_index("kv")
    spot = lax.axis_index("seq")
    tok = q_ref.shape[0]
    rows = tok * nk
    width = q_ref.shape[1] // nk
    peers = [lax.rem(me + o, nk) for o in range(1, nk)]
    ahead = [lax.rem(spot + d, ns) for d in range(1, WIN + 1)]
    behind = [lax.rem(spot + ns - d, ns) for d in range(1, WIN + 1)]

    barrier = pltpu.get_barrier_semaphore()
    for peer in peers:
        pl.semaphore_signal(barrier, inc=1, device_id={"kv": peer}, device_id_type=MESH)
    for peer in behind:
        pl.semaphore_signal(barrier, inc=1, device_id={"seq": peer}, device_id_type=MESH)
    pl.semaphore_wait(barrier, nk - 1 + WIN)

    mine = pl.ds(pl.multiple_of(me * tok, tok), tok)
    arrays = (
        (k_ref, kw.at[WIN], HD),
        (v_ref, vw.at[WIN], HD),
        (q_ref, q_out, width),
        (g_ref, g_out, width),
    )

    def piece(src, size, to):
        return src.at[:, pl.ds(pl.multiple_of(to * size, size), size)]

    copies = []
    locals_ = []
    for a, (src, dst, size) in enumerate(arrays):
        local = pltpu.make_async_copy(piece(src, size, me), dst.at[mine, :], own_sem.at[a])
        local.start()
        locals_.append(local)
        sent = []
        for o, peer in enumerate(peers):
            copy = remote(
                piece(src, size, peer), dst.at[mine, :], send_kv.at[a, o], recv_kv.at[a, o], {"kv": peer}
            )
            copy.start()
            sent.append(copy)
        copies.append(sent)
    far = []
    for a, win in enumerate((kw, vw)):
        locals_[a].wait()
        for copy in copies[a]:
            copy.wait_recv()
        for d in range(1, WIN + 1):
            copy = remote(
                win.at[WIN], win.at[WIN - d], send_win.at[a, d - 1], recv_win.at[a, d - 1], {"seq": ahead[d - 1]}
            )
            copy.start()
            far.append(copy)
    for a in (2, 3):
        locals_[a].wait()
        for copy in copies[a]:
            copy.wait_recv()
    for copy in far:
        copy.wait()
    for sent in copies:
        for copy in sent:
            copy.wait_send()


def gather(queries, keys, values, grad_out):
    nk, ns = lax.axis_size("kv"), lax.axis_size("seq")
    tok = queries.shape[0]
    rows = tok * nk
    width = queries.shape[1] // nk
    return pl.pallas_call(
        functools.partial(gather_kernel, nk, ns),
        out_shape=(
            jax.ShapeDtypeStruct((rows, width), BF16),
            jax.ShapeDtypeStruct((rows, width), BF16),
            jax.ShapeDtypeStruct((WIN + 1, rows, HD), BF16),
            jax.ShapeDtypeStruct((WIN + 1, rows, HD), BF16),
        ),
        in_specs=[any_spec()] * 4,
        out_specs=(vmem_spec(), vmem_spec(), vmem_spec(), vmem_spec()),
        scratch_shapes=[
            pltpu.SemaphoreType.DMA((4,)),
            pltpu.SemaphoreType.DMA((4, nk - 1)),
            pltpu.SemaphoreType.DMA((4, nk - 1)),
            pltpu.SemaphoreType.DMA((2, WIN)),
            pltpu.SemaphoreType.DMA((2, WIN)),
        ],
        compiler_params=pltpu.CompilerParams(
            collective_id=0, has_side_effects=True, vmem_limit_bytes=48 << 20
        ),
        name="gather",
    )(queries, keys, values, grad_out)


def dot(a, b):
    return jnp.dot(a, b, preferred_element_type=F32)


def dot_nt(a, b):
    return lax.dot_general(a, b, (((1,), (1,)), ((), ())), preferred_element_type=F32)


def fold(x, op):
    rows, cols = x.shape
    return op(x.reshape(rows // 8, 8, cols), axis=0)


def attend_kernel(
    first_ref, ends_ref, q_ref, g_ref, kw, vw, o_ref, dq_ref, dk_ref, dv_ref,
    bias, scores, probs, key_t, val_t, dk_acc, dv_acc,
):
    blocks, rows, _ = kw.shape
    first = first_ref[0]
    query_pos = first + lax.broadcasted_iota(jnp.int32, (1, rows), 1)
    start = jnp.zeros((1, rows), jnp.int32)
    for d in range(ends_ref.shape[0]):
        end = ends_ref[d]
        start = jnp.where(query_pos >= end, jnp.maximum(start, end), start)
    for b in range(blocks):
        key_pos = first + (b - WIN) * rows + lax.broadcasted_iota(jnp.int32, (rows, rows), 0)
        allowed = (key_pos >= start) & (key_pos <= query_pos)
        bias[b] = jnp.where(allowed, 0.0, MASKED)
        key_t[b] = kw[b].T
        val_t[b] = vw[b].T
        dk_acc[b] = jnp.zeros((rows, HD), F32)
        dv_acc[b] = jnp.zeros((rows, HD), F32)

    def step(h, carry):
        cols = pl.ds(pl.multiple_of(h * HD, HD), HD)
        qh = q_ref[:, cols]
        gh = g_ref[:, cols]
        top = jnp.full((8, rows), MASKED, F32)
        for b in range(blocks):
            s = dot_nt(kw[b], qh) + bias[b]
            scores[b] = s
            top = jnp.maximum(top, fold(s, jnp.max))
        top = jnp.max(top, axis=0, keepdims=True) * SCALE2
        total = jnp.zeros((8, rows), F32)
        out_t = jnp.zeros((HD, rows), F32)
        for b in range(blocks):
            p = jnp.exp2(scores[b] * SCALE2 - top)
            total = total + fold(p, jnp.sum)
            low = p.astype(BF16)
            probs[b] = low
            out_t = out_t + dot(val_t[b], low)
        over = 1.0 / jnp.sum(total, axis=0, keepdims=True)
        out_low = (out_t * over).T.astype(BF16)
        o_ref[:, cols] = out_low
        delta = jnp.sum((gh.astype(F32) * out_low.astype(F32)).T, axis=0, keepdims=True)
        over_col = jnp.broadcast_to(over, (HD, rows)).T
        qs = (qh.astype(F32) * over_col).astype(BF16)
        gs = (gh.astype(F32) * over_col).astype(BF16)
        dq_t = jnp.zeros((HD, rows), F32)
        for b in range(blocks):
            low = probs[b]
            ds = (low.astype(F32) * (dot_nt(vw[b], gh) - delta)).astype(BF16)
            dk_acc[b] += dot(ds, qs)
            dv_acc[b] += dot(low, gs)
            dq_t = dq_t + dot(key_t[b], ds)
        dq_ref[:, cols] = (dq_t * (over * SCALE)).T.astype(BF16)
        return carry

    lax.fori_loop(0, GROUP, step, 0)
    dk_ref[...] = dk_acc[...].astype(dk_ref.dtype)
    dv_ref[...] = dv_acc[...].astype(dv_ref.dtype)


def attend(q_loc, g_loc, kw, vw, first, ends):
    blocks, rows, _ = kw.shape
    smem = pl.BlockSpec(memory_space=pltpu.SMEM)
    return pl.pallas_call(
        attend_kernel,
        out_shape=(
            jax.ShapeDtypeStruct(q_loc.shape, BF16),
            jax.ShapeDtypeStruct(q_loc.shape, BF16),
            jax.ShapeDtypeStruct(kw.shape, BF16),
            jax.ShapeDtypeStruct(kw.shape, BF16),
        ),
        in_specs=[smem, smem] + [vmem_spec()] * 4,
        out_specs=(vmem_spec(),) * 4,
        scratch_shapes=[
            pltpu.VMEM((blocks, rows, rows), F32),
            pltpu.VMEM((blocks, rows, rows), F32),
            pltpu.VMEM((blocks, rows, rows), BF16),
            pltpu.VMEM((blocks, HD, rows), BF16),
            pltpu.VMEM((blocks, HD, rows), BF16),
            pltpu.VMEM((blocks, rows, HD), F32),
            pltpu.VMEM((blocks, rows, HD), F32),
        ],
        compiler_params=pltpu.CompilerParams(vmem_limit_bytes=48 << 20),
        name="attend",
    )(first, ends, q_loc, g_loc, kw, vw)


def scatter_kernel(
    nk, ns, o_ref, dq_ref, dkp, dvp, o_out, dq_out, dk_out, dv_out,
    held, summed, own_sem, send_kv, recv_kv, send_win, recv_win,
):
    me = lax.axis_index("kv")
    spot = lax.axis_index("seq")
    tok = o_out.shape[0]
    width = o_ref.shape[1]
    peers = [lax.rem(me + o, nk) for o in range(1, nk)]
    ahead = [lax.rem(spot + d, ns) for d in range(1, WIN + 1)]
    behind = [lax.rem(spot + ns - d, ns) for d in range(1, WIN + 1)]

    barrier = pltpu.get_barrier_semaphore()
    for peer in peers:
        pl.semaphore_signal(barrier, inc=1, device_id={"kv": peer}, device_id_type=MESH)
    for peer in ahead:
        pl.semaphore_signal(barrier, inc=1, device_id={"seq": peer}, device_id_type=MESH)
    pl.semaphore_wait(barrier, nk - 1 + WIN)

    far = []
    for a, part in enumerate((dkp, dvp)):
        for d in range(1, WIN + 1):
            copy = remote(
                part.at[WIN - d], held.at[a, d - 1], send_win.at[a, d - 1], recv_win.at[a, d - 1],
                {"seq": behind[d - 1]},
            )
            copy.start()
            far.append(copy)

    sends = []
    locals_ = []

    def spread(a, src, dst, size):
        def rows_of(to):
            return src.at[pl.ds(pl.multiple_of(to * tok, tok), tok), :]

        mine = dst.at[:, pl.ds(pl.multiple_of(me * size, size), size)]
        local = pltpu.make_async_copy(rows_of(me), mine, own_sem.at[a])
        local.start()
        locals_.append(local)
        for o, peer in enumerate(peers):
            copy = remote(rows_of(peer), mine, send_kv.at[a, o], recv_kv.at[a, o], {"kv": peer})
            copy.start()
            sends.append(copy)

    spread(0, o_ref, o_out, width)
    spread(1, dq_ref, dq_out, width)
    for a, (part, dst) in enumerate(((dkp, dk_out), (dvp, dv_out))):
        for copy in far[a * WIN:(a + 1) * WIN]:
            copy.wait_recv()
        total = part[WIN].astype(F32)
        for d in range(WIN):
            total = total + held[a, d].astype(F32)
        if a == 0:
            total = total * SCALE
        summed[a] = total.astype(BF16)
        spread(2 + a, summed.at[a], dst, HD)
    for local in locals_:
        local.wait()
    for copy in sends:
        copy.wait()
    for copy in far:
        copy.wait_send()


def scatter(o_loc, dq_loc, dkp, dvp):
    nk, ns = lax.axis_size("kv"), lax.axis_size("seq")
    rows, width = o_loc.shape
    tok = rows // nk
    return pl.pallas_call(
        functools.partial(scatter_kernel, nk, ns),
        out_shape=(
            jax.ShapeDtypeStruct((tok, width * nk), BF16),
            jax.ShapeDtypeStruct((tok, width * nk), BF16),
            jax.ShapeDtypeStruct((tok, HD * nk), BF16),
            jax.ShapeDtypeStruct((tok, HD * nk), BF16),
        ),
        in_specs=[vmem_spec()] * 4,
        out_specs=(any_spec(),) * 4,
        scratch_shapes=[
            pltpu.VMEM((2, WIN, rows, HD), BF16),
            pltpu.VMEM((2, rows, HD), BF16),
            pltpu.SemaphoreType.DMA((4,)),
            pltpu.SemaphoreType.DMA((4, nk - 1)),
            pltpu.SemaphoreType.DMA((4, nk - 1)),
            pltpu.SemaphoreType.DMA((2, WIN)),
            pltpu.SemaphoreType.DMA((2, WIN)),
        ],
        compiler_params=pltpu.CompilerParams(
            collective_id=1, has_side_effects=True, vmem_limit_bytes=48 << 20
        ),
        name="scatter",
    )(o_loc, dq_loc, dkp, dvp)


def body(queries, keys, values, grad_out, lengths):
    ends = jnp.cumsum(lengths).astype(jnp.int32)
    rows = queries.shape[0] * lax.axis_size("kv")
    first = (lax.axis_index("seq") * rows).astype(jnp.int32).reshape(1)
    q_loc, g_loc, kw, vw = gather(queries, keys, values, grad_out)
    o_loc, dq_loc, dkp, dvp = attend(q_loc, g_loc, kw, vw, first, ends)
    return scatter(o_loc, dq_loc, dkp, dvp)


def solution(mesh):
    split = P(("seq", "kv"), None)
    return jax.shard_map(
        body,
        mesh=mesh,
        in_specs=(split, split, split, split, P()),
        out_specs=(split, split, split, split),
        check_vma=False,
    )
```

time: 271 us -> 104 us (0.38)
  the two profiles are of different devices: /device:TPU:100 before, /device:TPU:5 now
where the time goes in v1:
time: 104 us
  Pallas kernels  96.3 us (93%)
  local copies, waits for them, and re-layouts  6.53 us (6%)
    pallas_call x1, Pallas kernels, scatter(): pl.pallas_call(functools.partial(scatter_kernel, nk, ns), out_shape=(jax....  41.1 us
    pallas_call x1, Pallas kernels, gather(): pl.pallas_call(functools.partial(gather_kernel, nk, ns), out_shape=(jax.S...  34.4 us
    pallas_call x1, Pallas kernels, attend(): pl.pallas_call(attend_kernel, out_shape=(jax.ShapeDtypeStruct(q_loc.shape...  20.8 us
    unnamed x12, local copies, waits for them, and re-layouts  5.77 us

profile of v1, /device:TPU:5, one launch (start us, length us, event | category | flops | bytes accessed | tf_op | source)
XLA Modules:
  0.0 103.7 jit_solution(11761434314764287301)
XLA Ops:
  0.6 0.0 copy-start.2
  0.6 0.8 copy.10
  1.4 0.1 reduce-window.9
  1.5 0.1 reduce.ends_ref
  1.6 0.0 copy-done.2
  1.6 0.0 copy-start
  1.6 1.0 copy-done
  2.6 0.0 copy-start.1
  2.6 1.0 %copy-done.1 = bf16[32,8192]{1,0:T(8,128)(2,1)S(1)} copy-done((bf16[32,8192]{1,0:T(8,128)(2,1)S(1)}, bf16[32,8192]{1,0:T(8,128)(2,1)}, u32[]{:S(2)}) %copy-start.1) | copy-done | bytes 524312
  3.7 0.0 copy-start.3
  3.7 0.8 copy-done.3
  4.5 34.4 %gather.1 = (bf16[256,1024]{1,0:T(8,128)(2,1)S(1)}, bf16[256,1024]{1,0:T(8,128)(2,1)S(1)}, bf16[7,256,128]{2,1,0:T(8,128)(2,1)S(1)}, bf16[7,256,128]{2,1,0:T(8,128)(2,1)S(1)}) custom-call(bf16[32,8192]{1,0:T(8,128)(2,1)S(1)} %copy-done, bf16[32,1024]{1,0:T(8,128)(2,1)S(1)} %copy-done.2, bf16[32,1024]{1,0:T(8,128)(2,1)S(1)} %copy-done.3, ...), custom_call_target="tpu_custom_call" | custom-call | tf_op jit(solution)/shard_map/gather/pallas_call | solution.py:104
  38.9 20.8 %attend.1 = (bf16[256,1024]{1,0:T(8,128)(2,1)S(1)}, bf16[256,1024]{1,0:T(8,128)(2,1)S(1)}, bf16[7,256,128]{2,1,0:T(8,128)(2,1)S(1)}, bf16[7,256,128]{2,1,0:T(8,128)(2,1)S(1)}) custom-call(s32[1]{0:T(128)} %bitcast.first_ref, s32[32]{0:T(128)S(1)} %reduce.ends_ref, bf16[256,1024]{1,0:T(8,128)(2,1)S(1)} %get-tuple-element.12.q_ref, ...), custom_call_target="tpu_custom_call" | custom-call | tf_op jit(solution)/shard_map/attend/pallas_call | solution.py:204
  59.7 41.1 %scatter.1 = (bf16[32,8192]{1,0:T(8,128)(2,1)S(1)}, bf16[32,8192]{1,0:T(8,128)(2,1)S(1)}, bf16[32,1024]{1,0:T(8,128)(2,1)S(1)}, bf16[32,1024]{1,0:T(8,128)(2,1)S(1)}) custom-call(bf16[256,1024]{1,0:T(8,128)(2,1)S(1)} %get-tuple-element.16.o_ref, bf16[256,1024]{1,0:T(8,128)(2,1)S(1)} %get-tuple-element.17.dq_ref, ...), custom_call_target="tpu_custom_call" | custom-call | tf_op jit(solution)/shard_map/scatter/pallas_call | solution.py:297
  100.8 0.8 copy.15
  101.6 0.8 copy.16
  102.4 0.6 copy.17
  103.1 0.6 copy.18
Async XLA Ops:
  0.6 1.0 copy-start.2
  1.6 1.0 %copy-start = (bf16[32,8192]{1,0:T(8,128)(2,1)S(1)}, bf16[32,8192]{1,0:T(8,128)(2,1)}, u32[]{:S(2)}) copy-start(bf16[32,8192]{1,0:T(8,128)(2,1)} %q_ref.1) | copy-start | bytes 1572868
  2.6 1.0 %copy-start.1 = (bf16[32,8192]{1,0:T(8,128)(2,1)S(1)}, bf16[32,8192]{1,0:T(8,128)(2,1)}, u32[]{:S(2)}) copy-start(bf16[32,8192]{1,0:T(8,128)(2,1)} %g_ref.1) | copy-start | bytes 1572868
  3.7 0.8 copy-start.3

commit v2 on v0

v2 whole, which is shorter than its diff:
```python
import functools

import jax
import jax.numpy as jnp
from jax import lax
from jax.experimental import pallas as pl
from jax.experimental.pallas import tpu as pltpu
from jax.sharding import PartitionSpec as P

HD = 128
GROUP = 8
WIN = 6
XS = 4
PIECES = 2
MESH = pl.DeviceIdType.MESH
SCALE = HD ** (-0.5)
SCALE2 = SCALE * 1.4426950408889634
MASKED = -1e30
F32 = jnp.float32
BF16 = jnp.bfloat16


def dot(a, b):
    return jnp.dot(a, b, preferred_element_type=F32)


def dot_nt(a, b):
    return lax.dot_general(a, b, (((1,), (1,)), ((), ())), preferred_element_type=F32)


def fold(x, op):
    rows, cols = x.shape
    return op(x.reshape(rows // 8, 8, cols), axis=0)


def span(i, size):
    return pl.ds(pl.multiple_of(i * size, size), size)


def kernel(
    nk, ns, lens_ref, q_ref, k_ref, v_ref, g_ref, o_out, dq_out, dk_out, dv_out,
    q_loc, g_loc, kwin, vwin, o_loc, dq_loc, part_k, part_v, held, moved, summed, final,
    bias, key_t, val_t, scores, probs, dscores, over, delta, qs, gs,
    own_sem, in_send, in_recv, win_send, win_recv, back_send, back_recv, out_send, out_recv,
):
    me = lax.axis_index("kv")
    spot = lax.axis_index("seq")
    col = lax.rem(spot, XS)
    tok = q_ref.shape[0]
    rows = tok * nk
    width = GROUP * HD
    peers = [lax.rem(me + o, nk) for o in range(1, nk)]

    def along(d):
        return {"seq": lax.rem(spot + ns + d, ns)}

    def beside(e):
        return {"seq": spot - col + lax.rem(col + XS + e, XS)}

    barrier = pltpu.get_barrier_semaphore()
    friends = [{"kv": p} for p in peers] + [beside(e) for e in (1, 2, 3)]
    friends += [along(s * d) for d in (1, 2, 3, 4, 8) for s in (1, -1)]
    for friend in friends:
        pl.semaphore_signal(barrier, inc=1, device_id=friend, device_id_type=MESH)
    pl.semaphore_wait(barrier, len(friends))

    def remote(src, dst, send, recv, peer):
        return pltpu.make_async_remote_copy(
            src_ref=src, dst_ref=dst, send_sem=send, recv_sem=recv, device_id=peer, device_id_type=MESH
        )

    pending, leaving = [], []


    def collect(a, src, dst, base, size):
        place = pl.ds(pl.multiple_of(base + me * tok, tok), tok)
        local = pltpu.make_async_copy(src.at[:, span(me, size)], dst.at[place, :], own_sem.at[a])
        local.start()
        got = [local]
        for o, peer in enumerate(peers):
            copy = remote(src.at[:, span(peer, size)], dst.at[place, :], in_send.at[a, o], in_recv.at[a, o], {"kv": peer})
            copy.start()
            leaving.append(copy)
            got.append(copy)
        return got

    def arrive(got):
        got[0].wait()
        for copy in got[1:]:
            copy.wait_recv()

    got_k = collect(0, k_ref, kwin, WIN * rows, HD)
    got_v = collect(1, v_ref, vwin, WIN * rows, HD)
    got_q = collect(2, q_ref, q_loc, 0, width)

    first = spot * rows
    query_pos = first + lax.broadcasted_iota(jnp.int32, (1, rows), 1)
    start = jnp.zeros((1, rows), jnp.int32)
    end = jnp.int32(0)
    for d in range(lens_ref.shape[0]):
        end = end + lens_ref[d]
        start = jnp.where(query_pos >= end, end, start)
    for b in range(WIN + 1):
        key_pos = first + (b - WIN) * rows + lax.broadcasted_iota(jnp.int32, (rows, rows), 0)
        allowed = key_pos >= start
        if b == WIN:
            allowed = allowed & (key_pos <= query_pos)
        bias[b] = jnp.where(allowed, 0.0, MASKED)

    def slot(win, i):
        return win.at[pl.ds(i * rows, rows), :]

    def share(a, win):
        copies = {}
        for d in (4, 8, 3, 2, 1):
            i = 7 if d == 8 else WIN - d
            copy = remote(slot(win, WIN), slot(win, i), win_send.at[a, i], win_recv.at[a, i], along(d))
            copies[d] = copy
            if d == 8:
                @pl.when(col >= 2)
                def _():
                    copy.start()
            else:
                copy.start()
        return copies

    def relay(a, win, copies):
        copies[4].wait_recv()

        @pl.when(col >= 2)
        def _():
            copies[8].wait_recv()

        for e in (2, 1):
            i = WIN - 4 - e
            from_slot = jnp.where(col + e >= XS, 7, WIN - 4)
            copy = remote(
                win.at[span(from_slot, rows), :], slot(win, i), win_send.at[a, i], win_recv.at[a, i], beside(e)
            )
            copy.start()
            copies[4 + e] = copy

    def landed(copies):
        for d in (1, 2, 3, 5, 6):
            copies[d].wait_recv()

    arrive(got_k)
    far_k = share(0, kwin)
    arrive(got_v)
    far_v = share(1, vwin)
    got_g = collect(3, g_ref, g_loc, 0, width)
    relay(0, kwin, far_k)
    relay(1, vwin, far_v)
    landed(far_k)
    arrive(got_q)

    def head(h):
        return span(h, HD)

    def score_step(h, carry):
        qh = q_loc[:, head(h)]
        top = jnp.full((8, rows), MASKED, F32)
        for b in range(WIN + 1):
            s = dot_nt(kwin[b * rows:(b + 1) * rows], qh) + bias[b]
            scores[b] = s
            top = jnp.maximum(top, fold(s, jnp.max))
        top = jnp.max(top, axis=0, keepdims=True) * SCALE2
        total = jnp.zeros((8, rows), F32)
        for b in range(WIN + 1):
            p = jnp.exp2(scores[b] * SCALE2 - top)
            total = total + fold(p, jnp.sum)
            probs[h, b * rows:(b + 1) * rows] = p.astype(BF16)
        over[pl.ds(h, 1), :] = 1.0 / jnp.sum(total, axis=0, keepdims=True)
        return carry

    lax.fori_loop(0, GROUP, score_step, 0)

    for b in range(WIN + 1):
        key_t[:, b * rows:(b + 1) * rows] = kwin[b * rows:(b + 1) * rows].T
    landed(far_v)
    for b in range(WIN + 1):
        val_t[:, b * rows:(b + 1) * rows] = vwin[b * rows:(b + 1) * rows].T
    arrive(got_g)

    def spread(a, src, dst, base, size, wide):
        def rows_of(to):
            return src.at[span(to, tok), pl.ds(base, size)]

        mine = dst.at[:, pl.ds(pl.multiple_of(me * wide + base, HD), size)]
        local = pltpu.make_async_copy(rows_of(me), mine, own_sem.at[4 + a])
        local.start()
        pending.append(local)
        for o, peer in enumerate(peers):
            copy = remote(rows_of(peer), mine, out_send.at[a, o], out_recv.at[a, o], {"kv": peer})
            copy.start()
            pending.append(copy)

    def out_step(h, carry):
        inv = over[pl.ds(h, 1), :]
        qh = q_loc[:, head(h)]
        gh = g_loc[:, head(h)]
        low = (dot(val_t[...], probs[h]) * inv).T.astype(BF16)
        o_loc[:, head(h)] = low
        delta[pl.ds(h, 1), :] = jnp.sum((gh.astype(F32) * low.astype(F32)).T, axis=0, keepdims=True)
        inv_col = jnp.broadcast_to(inv, (HD, rows)).T
        qs[span(h, rows), :] = (qh.astype(F32) * inv_col).astype(BF16)
        gs[span(h, rows), :] = (gh.astype(F32) * inv_col).astype(BF16)
        return carry

    each = GROUP // PIECES
    for i in range(PIECES):
        lax.fori_loop(i * each, (i + 1) * each, out_step, 0, unroll=2)
        spread(i, o_loc, o_out, i * each * HD, each * HD, width)

    back = {}

    def give(a, part, b):
        d = WIN - b
        peer = along(-d) if d <= 3 else beside(4 - d)
        copy = remote(part.at[b], held.at[a, b], back_send.at[a, b], back_recv.at[a, b], peer)
        copy.start()
        back[a, d] = copy

    def pass_on(a, part):
        back[a, 5].wait_recv()
        back[a, 6].wait_recv()
        far5, far6 = held[a, WIN - 5].astype(F32), held[a, WIN - 6].astype(F32)
        wrap5 = jnp.where(col >= 3, 1.0, 0.0)
        wrap6 = jnp.where(col >= 2, 1.0, 0.0)
        moved[a, 0] = (part[WIN - 4].astype(F32) + far5 * (1.0 - wrap5) + far6 * (1.0 - wrap6)).astype(BF16)
        moved[a, 1] = (far5 * wrap5 + far6 * wrap6).astype(BF16)
        i = WIN - 4
        copy = remote(moved.at[a, 0], held.at[a, i], back_send.at[a, i], back_recv.at[a, i], along(-4))
        copy.start()
        back[a, 4] = copy
        deep = remote(moved.at[a, 1], held.at[a, WIN], back_send.at[a, WIN], back_recv.at[a, WIN], along(-8))
        back[a, 8] = deep

        @pl.when(col >= 2)
        def _():
            deep.start()

    def finish(a, part, factor, dst):
        total = part[WIN].astype(F32)
        for d in (1, 2, 3, 4):
            back[a, d].wait_recv()
            total = total + held[a, WIN - d].astype(F32)
        summed[a] = total

        @pl.when(col >= 2)
        def _():
            back[a, 8].wait_recv()
            summed[a] = summed[a] + held[a, WIN].astype(F32)

        final[a] = (summed[a] * factor).astype(BF16)
        spread(2 * PIECES + a, final.at[a], dst, 0, HD, HD)

    for b in range(WIN + 1):
        block = slice(b * rows, (b + 1) * rows)

        def dv_step(h, acc):
            return acc + dot(probs[h, block], gs[span(h, rows), :])

        acc = lax.fori_loop(0, GROUP, dv_step, jnp.zeros((rows, HD), F32), unroll=True)
        part_v[b] = acc.astype(BF16)
        if b < WIN and b != WIN - 4:
            give(1, part_v, b)

    for b in range(WIN + 1):
        block = slice(b * rows, (b + 1) * rows)
        vb = vwin[block]

        def dk_step(h, acc):
            dp = dot_nt(vb, g_loc[:, head(h)])
            ds = (probs[h, block].astype(F32) * (dp - delta[pl.ds(h, 1), :])).astype(BF16)
            dscores[h, block] = ds
            return acc + dot(ds, qs[span(h, rows), :])

        acc = lax.fori_loop(0, GROUP, dk_step, jnp.zeros((rows, HD), F32), unroll=True)
        part_k[b] = acc.astype(BF16)
        if b < WIN and b != WIN - 4:
            give(0, part_k, b)
        if b == 2:
            pass_on(1, part_v)
    pass_on(0, part_k)

    def dq_step(h, carry):
        dq_t = dot(key_t[...], dscores[h])
        dq_loc[:, head(h)] = (dq_t * (over[pl.ds(h, 1), :] * SCALE)).T.astype(BF16)
        return carry

    for i in range(PIECES):
        lax.fori_loop(i * each, (i + 1) * each, dq_step, 0, unroll=2)
        spread(PIECES + i, dq_loc, dq_out, i * each * HD, each * HD, width)

    finish(1, part_v, 1.0, dv_out)
    finish(0, part_k, SCALE, dk_out)

    for copy in leaving:
        copy.wait_send()
    for copies in (far_k, far_v):
        for d, copy in copies.items():
            if d != 8:
                copy.wait_send()
    for (a, d), copy in back.items():
        if d != 8:
            copy.wait_send()

    @pl.when(col >= 2)
    def _():
        for copy in (far_k[8], far_v[8], back[0, 8], back[1, 8]):
            copy.wait_send()

    for copy in pending:
        copy.wait()


def body(queries, keys, values, grad_out, lengths):
    nk, ns = lax.axis_size("kv"), lax.axis_size("seq")
    tok = queries.shape[0]
    rows = tok * nk
    width = GROUP * HD
    blocks = WIN + 1
    whole = pl.BlockSpec(memory_space=pl.ANY)
    dma = pltpu.SemaphoreType.DMA
    return pl.pallas_call(
        functools.partial(kernel, nk, ns),
        out_shape=(
            jax.ShapeDtypeStruct(queries.shape, BF16),
            jax.ShapeDtypeStruct(queries.shape, BF16),
            jax.ShapeDtypeStruct(keys.shape, BF16),
            jax.ShapeDtypeStruct(keys.shape, BF16),
        ),
        in_specs=[pl.BlockSpec(memory_space=pltpu.SMEM)] + [whole] * 4,
        out_specs=(whole,) * 4,
        scratch_shapes=[
            pltpu.VMEM((rows, width), BF16),
            pltpu.VMEM((rows, width), BF16),
            pltpu.VMEM(((blocks + 1) * rows, HD), BF16),
            pltpu.VMEM(((blocks + 1) * rows, HD), BF16),
            pltpu.VMEM((rows, width), BF16),
            pltpu.VMEM((rows, width), BF16),
            pltpu.VMEM((blocks, rows, HD), BF16),
            pltpu.VMEM((blocks, rows, HD), BF16),
            pltpu.VMEM((2, blocks, rows, HD), BF16),
            pltpu.VMEM((2, 2, rows, HD), BF16),
            pltpu.VMEM((2, rows, HD), F32),
            pltpu.VMEM((2, rows, HD), BF16),
            pltpu.VMEM((blocks, rows, rows), F32),
            pltpu.VMEM((HD, blocks * rows), BF16),
            pltpu.VMEM((HD, blocks * rows), BF16),
            pltpu.VMEM((blocks, rows, rows), F32),
            pltpu.VMEM((GROUP, blocks * rows, rows), BF16),
            pltpu.VMEM((GROUP, blocks * rows, rows), BF16),
            pltpu.VMEM((GROUP, rows), F32),
            pltpu.VMEM((GROUP, rows), F32),
            pltpu.VMEM((GROUP * rows, HD), BF16),
            pltpu.VMEM((GROUP * rows, HD), BF16),
            dma((4 + 2 * PIECES + 2,)),
            dma((4, nk - 1)),
            dma((4, nk - 1)),
            dma((2, 8)),
            dma((2, 8)),
            dma((2, blocks)),
            dma((2, blocks)),
            dma((2 * PIECES + 2, nk - 1)),
            dma((2 * PIECES + 2, nk - 1)),
        ],
        compiler_params=pltpu.CompilerParams(
            collective_id=0, has_side_effects=True, vmem_limit_bytes=60 << 20
        ),
        name="attend",
    )(lengths, queries, keys, values, grad_out)


def solution(mesh):
    split = P(("seq", "kv"), None)
    return jax.shard_map(
        body,
        mesh=mesh,
        in_specs=(split, split, split, split, P()),
        out_specs=(split, split, split, split),
        check_vma=False,
    )
```

time: 271 us -> 70.5 us (0.26)
  the two profiles are of different devices: /device:TPU:100 before, /device:TPU:1 now
where the time goes in v2:
time: 70.5 us; the launch traced here: 70.3 us
  Pallas kernels  65.3 us (93%)
  local copies, waits for them, and re-layouts  4.28 us (6%)
    pallas_call x1, Pallas kernels, body(): pl.pallas_call(functools.partial(kernel, nk, ns), out_shape=(jax.ShapeDty...  65.3 us
    unnamed x10, local copies, waits for them, and re-layouts  4.28 us

profile of v2, /device:TPU:1, one launch (start us, length us, event | category | flops | bytes accessed | tf_op | source)
XLA Modules:
  0.0 70.3 jit_solution(1303807906042711969)
XLA Ops:
  0.6 65.3 %attend.1 = (bf16[32,8192]{1,0:T(8,128)(2,1)}, bf16[32,8192]{1,0:T(8,128)(2,1)}, bf16[32,1024]{1,0:T(8,128)(2,1)}, bf16[32,1024]{1,0:T(8,128)(2,1)}) custom-call(s32[32]{0:T(128)} %lens_ref.1, bf16[32,8192]{1,0:T(8,128)(2,1)} %q_ref.1, bf16[32,1024]{1,0:T(8,128)(2,1)} %k_ref.1, bf16[32,1024]{1,0:T(8,128)(2,1)} %v_ref.1, bf16[32,8192]{1,0:T(8,128)(2,1)} %g_ref.1), custom_call_target="tpu_custom_call" | custom-call | tf_op jit(solution)/shard_map/attend/pallas_call | solution.py:326
  66.0 0.0 copy-start
  66.0 1.9 %copy.13 = bf16[32,8192]{1,0:T(8,128)(2,1)} copy(bf16[32,8192]{1,0:T(8,128)(2,1)} %get-tuple-element.8) | data formatting | bytes 1048576
  67.9 0.0 copy-done
  67.9 0.0 copy-start.2
  67.9 0.8 %copy.14 = bf16[32,8192]{1,0:T(8,128)(2,1)} copy(bf16[32,8192]{1,0:T(8,128)(2,1)S(1)} %copy-done) | data formatting | bytes 1048576
  68.7 0.1 copy-done.2
  68.8 0.0 copy-start.1
  68.8 0.6 copy.15
  69.4 0.2 copy-done.1
  69.6 0.6 copy.16
Async XLA Ops:
  66.0 1.9 %copy-start = (bf16[32,8192]{1,0:T(8,128)(2,1)S(1)}, bf16[32,8192]{1,0:T(8,128)(2,1)}, u32[]{:S(2)}) copy-start(bf16[32,8192]{1,0:T(8,128)(2,1)} %get-tuple-element.9) | copy-start | bytes 1572868
  67.9 0.9 %copy-start.2 = (bf16[32,1024]{1,0:T(8,128)(2,1)S(1)}, bf16[32,1024]{1,0:T(8,128)(2,1)}, u32[]{:S(2)}) copy-start(bf16[32,1024]{1,0:T(8,128)(2,1)} %get-tuple-element.10) | copy-start | bytes 196612
  68.8 0.9 %copy-start.1 = (bf16[32,1024]{1,0:T(8,128)(2,1)S(1)}, bf16[32,1024]{1,0:T(8,128)(2,1)}, u32[]{:S(2)}) copy-start(bf16[32,1024]{1,0:T(8,128)(2,1)} %get-tuple-element.11) | copy-start | bytes 196612

commit v3 on v2

v3 whole, which is shorter than its diff:
```python
import functools

import jax
import jax.numpy as jnp
from jax import lax
from jax.experimental import pallas as pl
from jax.experimental.pallas import tpu as pltpu
from jax.sharding import PartitionSpec as P

HD = 128
GROUP = 8
WIN = 6
XS = 4
CUTS = (0, 5, 8)
MESH = pl.DeviceIdType.MESH
SCALE = HD ** (-0.5)
SCALE2 = SCALE * 1.4426950408889634
MASKED = -1e30
F32 = jnp.float32
BF16 = jnp.bfloat16


def dot(a, b):
    return jnp.dot(a, b, preferred_element_type=F32)


def dot_nt(a, b):
    return lax.dot_general(a, b, (((1,), (1,)), ((), ())), preferred_element_type=F32)


def fold(x, op):
    rows, cols = x.shape
    return op(x.reshape(rows // 8, 8, cols), axis=0)


def span(i, size):
    return pl.ds(pl.multiple_of(i * size, size), size)


def kernel(
    nk, ns, lens_ref, q_ref, k_ref, v_ref, g_ref, o_out, dq_out, dk_out, dv_out,
    q_loc, g_loc, kwin, vwin, o_loc, dq_loc, part_k, part_v, held, moved, summed, final,
    bias, key_t, val_t, scores, tops, probs, dscores, over, delta, qs, gs,
    own_sem, in_send, in_recv, win_send, win_recv, back_send, back_recv, deep_send, deep_recv, out_send, out_recv,
):
    me = lax.axis_index("kv")
    spot = lax.axis_index("seq")
    col = lax.rem(spot, XS)
    tok = q_ref.shape[0]
    rows = tok * nk
    width = GROUP * HD
    peers = [lax.rem(me + o, nk) for o in range(1, nk)]

    def along(d):
        return {"seq": lax.rem(spot + ns + d, ns)}

    def beside(e):
        return {"seq": spot - col + lax.rem(col + XS + e, XS)}

    barrier = pltpu.get_barrier_semaphore()
    friends = [{"kv": p} for p in peers] + [beside(e) for e in (1, 2, 3)] + [along(XS), along(-XS)]
    for friend in friends:
        pl.semaphore_signal(barrier, inc=1, device_id=friend, device_id_type=MESH)
    pl.semaphore_wait(barrier, len(friends))

    def remote(src, dst, send, recv, peer):
        return pltpu.make_async_remote_copy(
            src_ref=src, dst_ref=dst, send_sem=send, recv_sem=recv, device_id=peer, device_id_type=MESH
        )

    pending, leaving = [], []


    def collect(a, src, dst, base, size):
        place = pl.ds(pl.multiple_of(base + me * tok, tok), tok)
        local = pltpu.make_async_copy(src.at[:, span(me, size)], dst.at[place, :], own_sem.at[a])
        local.start()
        for peer in peers:
            remote(
                src.at[:, span(peer, size)], dst.at[place, :], in_send.at[a], in_recv.at[a], {"kv": peer}
            ).start()
        n = nk - 1
        every = remote(
            src.at[:, pl.ds(0, n * size)], dst.at[pl.ds(base, n * tok), :], in_send.at[a], in_recv.at[a], {"kv": peers[0]}
        )
        leaving.append(every)
        return local, every

    def arrive(got):
        got[0].wait()
        got[1].wait_recv()

    got_k = collect(0, k_ref, kwin, WIN * rows, HD)
    got_v = collect(1, v_ref, vwin, WIN * rows, HD)
    got_q = collect(2, q_ref, q_loc, 0, width)
    got_g = collect(3, g_ref, g_loc, 0, width)

    first = spot * rows
    query_pos = first + lax.broadcasted_iota(jnp.int32, (1, rows), 1)
    start = jnp.zeros((1, rows), jnp.int32)
    end = jnp.int32(0)
    for d in range(lens_ref.shape[0]):
        end = end + lens_ref[d]
        start = jnp.where(query_pos >= end, end, start)
    for b in range(WIN + 1):
        key_pos = first + (b - WIN) * rows + lax.broadcasted_iota(jnp.int32, (rows, rows), 0)
        allowed = key_pos >= start
        if b == WIN:
            allowed = allowed & (key_pos <= query_pos)
        bias[b] = jnp.where(allowed, 0.0, MASKED)

    def slot(win, i):
        return win.at[pl.ds(i * rows, rows), :]

    def start_if(cond, copy):
        @pl.when(cond)
        def _():
            copy.start()

    def share(a, win):
        def hop(src, i, peer):
            return remote(src, slot(win, i), win_send.at[a, 1 if i == 7 else 0], win_recv.at[a, i], peer)

        copies = {4: hop(slot(win, WIN), WIN - 4, along(XS)), 8: hop(slot(win, WIN - 4), 7, along(XS))}
        for e in (2, 1, 3):
            near = jnp.where(col + e >= XS, WIN - 4, WIN)
            copies[e] = hop(win.at[span(near, rows), :], WIN - e, beside(e))
        for e in (2, 1):
            near = jnp.where(col + e >= XS, 7, WIN - 4)
            copies[4 + e] = hop(win.at[span(near, rows), :], WIN - 4 - e, beside(e))
        copies[4].start()
        for e in (2, 1, 3):
            start_if(col + e < XS, copies[e])
        return copies

    def relay(copies):
        copies[4].wait_recv()
        start_if(col >= 2, copies[8])
        for e in (2, 1, 3):
            start_if(col + e >= XS, copies[e])
        for e in (2, 1):
            start_if(col + e < XS, copies[4 + e])

    def relay_deep(copies):
        @pl.when(col >= 2)
        def _():
            copies[8].wait_recv()

        for e in (2, 1):
            start_if(col + e >= XS, copies[4 + e])

    def head(h):
        return span(h, HD)

    def score(b):
        block = slice(b * rows, (b + 1) * rows)

        def step(h, carry):
            s = dot_nt(kwin[block], q_loc[:, head(h)]) + bias[b]
            scores[h, block] = s
            top = fold(s, jnp.max)
            if b != WIN:
                top = jnp.maximum(top, tops[h])
            tops[h] = top
            return carry

        lax.fori_loop(0, GROUP, step, 0, unroll=4)

    arrive(got_k)
    far_k = share(0, kwin)
    arrive(got_v)
    far_v = share(1, vwin)
    relay(far_k)
    relay(far_v)
    arrive(got_q)
    score(WIN)
    relay_deep(far_k)
    relay_deep(far_v)
    for d in (1, 2, 3, 4, 5, 6):
        if d != 4:
            far_k[d].wait_recv()
        score(WIN - d)

    def weight_step(h, carry):
        top = jnp.max(tops[h], axis=0, keepdims=True) * SCALE2
        total = jnp.zeros((8, rows), F32)
        for b in range(WIN + 1):
            block = slice(b * rows, (b + 1) * rows)
            p = jnp.exp2(scores[h, block] * SCALE2 - top)
            total = total + fold(p, jnp.sum)
            probs[h, block] = p.astype(BF16)
        over[pl.ds(h, 1), :] = 1.0 / jnp.sum(total, axis=0, keepdims=True)
        return carry

    lax.fori_loop(0, GROUP, weight_step, 0)
    arrive(got_g)

    def scale_step(h, carry):
        inv_col = jnp.broadcast_to(over[pl.ds(h, 1), :], (HD, rows)).T
        qs[span(h, rows), :] = (q_loc[:, head(h)].astype(F32) * inv_col).astype(BF16)
        gs[span(h, rows), :] = (g_loc[:, head(h)].astype(F32) * inv_col).astype(BF16)
        return carry

    lax.fori_loop(0, GROUP, scale_step, 0, unroll=2)

    def spread(a, src, dst, base, size, wide):
        def rows_of(to):
            return src.at[span(to, tok), pl.ds(base, size)]

        mine = dst.at[:, pl.ds(pl.multiple_of(me * wide + base, HD), size)]
        local = pltpu.make_async_copy(rows_of(me), mine, own_sem.at[4 + a])
        local.start()
        pending.append(local)
        for peer in peers:
            remote(rows_of(peer), mine, out_send.at[a], out_recv.at[a], {"kv": peer}).start()
        n = nk - 1
        pending.append(
            remote(
                src.at[pl.ds(0, n * tok), pl.ds(base, size)], dst.at[:, pl.ds(0, n * size)],
                out_send.at[a], out_recv.at[a], {"kv": peers[0]},
            )
        )

    def out_step(h, carry):
        inv = over[pl.ds(h, 1), :]
        gh = g_loc[:, head(h)]
        low = (dot(val_t[...], probs[h]) * inv).T.astype(BF16)
        o_loc[:, head(h)] = low
        delta[pl.ds(h, 1), :] = jnp.sum((gh.astype(F32) * low.astype(F32)).T, axis=0, keepdims=True)
        return carry

    back = {}

    def give(a, part, b):
        d = WIN - b
        peer = beside(-d if d <= 3 else 4 - d)
        copy = remote(part.at[b], held.at[a, b], back_send.at[a], back_recv.at[a, b], peer)
        copy.start()
        back[a, d] = copy

    def send_on(a, i):
        copy = remote(moved.at[a, i], held.at[a, (WIN - 4, WIN)[i]], deep_send.at[a, i], deep_recv.at[a, i], along(-XS))
        back[a, (4, 8)[i]] = copy
        return copy

    def wrapped(e):
        return jnp.where(col + e >= XS, 1.0, 0.0)

    def pass_deep(a):
        back[a, 5].wait_recv()
        back[a, 6].wait_recv()
        deep = send_on(a, 1)

        @pl.when(col >= 2)
        def _():
            moved[a, 1] = (
                held[a, WIN - 5].astype(F32) * wrapped(1) + held[a, WIN - 6].astype(F32) * wrapped(2)
            ).astype(BF16)
            deep.start()

    def pass_on(a, part):
        total = part[WIN - 4].astype(F32)
        for e in (1, 2):
            total = total + held[a, WIN - 4 - e].astype(F32) * (1.0 - wrapped(e))
        for e in (1, 2, 3):
            back[a, e].wait_recv()
            total = total + held[a, WIN - e].astype(F32) * wrapped(e)
        summed[a] = total

        @pl.when(col >= 2)
        def _():
            back[a, 8].wait_recv()
            summed[a] = summed[a] + held[a, WIN].astype(F32)

        moved[a, 0] = summed[a].astype(BF16)
        send_on(a, 0).start()

    def finish(a, part, factor, dst):
        total = part[WIN].astype(F32)
        for e in (1, 2, 3):
            total = total + held[a, WIN - e].astype(F32) * (1.0 - wrapped(e))
        back[a, 4].wait_recv()
        total = total + held[a, WIN - 4].astype(F32)
        final[a] = (total * factor).astype(BF16)
        spread(len(CUTS) + a, final.at[a], dst, 0, HD, HD)

    order = (0, 1, 3, 4, 5, 2, 6)
    for b in order:
        block = slice(b * rows, (b + 1) * rows)

        def dv_step(h, acc):
            return acc + dot(probs[h, block], gs[span(h, rows), :])

        acc = lax.fori_loop(0, GROUP, dv_step, jnp.zeros((rows, HD), F32), unroll=True)
        part_v[b] = acc.astype(BF16)
        if b < WIN and b != WIN - 4:
            give(1, part_v, b)

    for d in (1, 2, 3, 5, 6):
        far_v[d].wait_recv()
    for b in range(WIN + 1):
        block = slice(b * rows, (b + 1) * rows)
        val_t[:, block] = vwin[block].T
    lax.fori_loop(0, GROUP, out_step, 0, unroll=2)
    spread(0, o_loc, o_out, 0, width, width)
    pass_deep(1)

    for b in order:
        block = slice(b * rows, (b + 1) * rows)
        vb = vwin[block]

        def dk_step(h, acc):
            dp = dot_nt(vb, g_loc[:, head(h)])
            ds = (probs[h, block].astype(F32) * (dp - delta[pl.ds(h, 1), :])).astype(BF16)
            dscores[h, block] = ds
            return acc + dot(ds, qs[span(h, rows), :])

        acc = lax.fori_loop(0, GROUP, dk_step, jnp.zeros((rows, HD), F32), unroll=True)
        part_k[b] = acc.astype(BF16)
        if b < WIN and b != WIN - 4:
            give(0, part_k, b)
        if b == 1:
            pass_on(1, part_v)
        if b == 2:
            pass_deep(0)
    finish(1, part_v, 1.0, dv_out)

    def dq_step(h, carry):
        dq_t = dot(key_t[...], dscores[h])
        dq_loc[:, head(h)] = (dq_t * (over[pl.ds(h, 1), :] * SCALE)).T.astype(BF16)
        return carry

    for b in range(WIN + 1):
        block = slice(b * rows, (b + 1) * rows)
        key_t[:, block] = kwin[block].T
    for i, (low, high) in enumerate(zip(CUTS, CUTS[1:])):
        lax.fori_loop(low, high, dq_step, 0, unroll=True)
        spread(1 + i, dq_loc, dq_out, low * HD, (high - low) * HD, width)
        if i == 0:
            pass_on(0, part_k)
    finish(0, part_k, SCALE, dk_out)

    for copy in leaving:
        copy.wait_send()
    for a, win in enumerate((kwin, vwin)):
        six = win.at[pl.ds(0, WIN * rows), :]
        remote(six, six, win_send.at[a, 0], win_recv.at[a, 0], along(XS)).wait_send()
    for a, part in enumerate((part_k, part_v)):
        five = part.at[pl.ds(0, WIN - 1)]
        remote(five, five, back_send.at[a], back_recv.at[a, 0], along(XS)).wait_send()
        back[a, 4].wait_send()

    @pl.when(col >= 2)
    def _():
        for copy in (far_k[8], far_v[8], back[0, 8], back[1, 8]):
            copy.wait_send()

    for copy in pending:
        copy.wait()


def hand_over(*refs):
    given, taken, held, sems = refs[:4], refs[4:8], refs[8:12], refs[12]
    come = [pltpu.make_async_copy(given[i], held[i], sems.at[0, i]) for i in range(4)]
    go = [pltpu.make_async_copy(held[i], taken[i], sems.at[1, i]) for i in range(4)]
    for copy in come:
        copy.start()
    for i in range(4):
        come[i].wait()
        go[i].start()
    for copy in go:
        copy.wait()


def body(queries, keys, values, grad_out, lengths):
    nk, ns = lax.axis_size("kv"), lax.axis_size("seq")
    tok = queries.shape[0]
    rows = tok * nk
    width = GROUP * HD
    blocks = WIN + 1
    whole = pl.BlockSpec(memory_space=pl.ANY)
    dma = pltpu.SemaphoreType.DMA
    results = pl.pallas_call(
        functools.partial(kernel, nk, ns),
        out_shape=(
            jax.ShapeDtypeStruct(queries.shape, BF16),
            jax.ShapeDtypeStruct(queries.shape, BF16),
            jax.ShapeDtypeStruct(keys.shape, BF16),
            jax.ShapeDtypeStruct(keys.shape, BF16),
        ),
        in_specs=[pl.BlockSpec(memory_space=pltpu.SMEM)] + [whole] * 4,
        out_specs=(whole,) * 4,
        scratch_shapes=[
            pltpu.VMEM((rows, width), BF16),
            pltpu.VMEM((rows, width), BF16),
            pltpu.VMEM(((blocks + 1) * rows, HD), BF16),
            pltpu.VMEM(((blocks + 1) * rows, HD), BF16),
            pltpu.VMEM((rows, width), BF16),
            pltpu.VMEM((rows, width), BF16),
            pltpu.VMEM((blocks, rows, HD), BF16),
            pltpu.VMEM((blocks, rows, HD), BF16),
            pltpu.VMEM((2, blocks, rows, HD), BF16),
            pltpu.VMEM((2, 2, rows, HD), BF16),
            pltpu.VMEM((2, rows, HD), F32),
            pltpu.VMEM((2, rows, HD), BF16),
            pltpu.VMEM((blocks, rows, rows), F32),
            pltpu.VMEM((HD, blocks * rows), BF16),
            pltpu.VMEM((HD, blocks * rows), BF16),
            pltpu.VMEM((GROUP, blocks * rows, rows), F32),
            pltpu.VMEM((GROUP, 8, rows), F32),
            pltpu.VMEM((GROUP, blocks * rows, rows), BF16),
            pltpu.VMEM((GROUP, blocks * rows, rows), BF16),
            pltpu.VMEM((GROUP, rows), F32),
            pltpu.VMEM((GROUP, rows), F32),
            pltpu.VMEM((GROUP * rows, HD), BF16),
            pltpu.VMEM((GROUP * rows, HD), BF16),
            dma((4 + len(CUTS) + 2,)),
            dma((4,)),
            dma((4,)),
            dma((2, 2)),
            dma((2, 8)),
            dma((2,)),
            dma((2, blocks)),
            dma((2, 2)),
            dma((2, 2)),
            dma((len(CUTS) + 2,)),
            dma((len(CUTS) + 2,)),
        ],
        compiler_params=pltpu.CompilerParams(
            collective_id=0, has_side_effects=True, vmem_limit_bytes=60 << 20
        ),
        name="attend",
    )(lengths, queries, keys, values, grad_out)
    return pl.pallas_call(
        hand_over,
        out_shape=tuple(jax.ShapeDtypeStruct(x.shape, x.dtype) for x in results),
        in_specs=[whole] * 4,
        out_specs=(whole,) * 4,
        scratch_shapes=[pltpu.VMEM(x.shape, x.dtype) for x in results] + [dma((2, 4))],
        compiler_params=pltpu.CompilerParams(vmem_limit_bytes=60 << 20),
        name="hand_over",
    )(*results)


def solution(mesh):
    split = P(("seq", "kv"), None)
    return jax.shard_map(
        body,
        mesh=mesh,
        in_specs=(split, split, split, split, P()),
        out_specs=(split, split, split, split),
        check_vma=False,
    )
```

time: 70.5 us -> 64.9 us (0.921)
  local copies, waits for them, and re-layouts: 4.28 us -> 0 us
  Pallas kernels: 65.3 us -> 63.9 us
    unnamed x10 -> x0, local copies, waits for them, and re-layouts: 4.28 us -> none
    pallas_call x1, Pallas kernels: 65.3 us -> 61.8 us  [body(): pl.pallas_call(functools.partial(kernel, nk, ns), out_shape=(jax.ShapeDty...]
    pallas_call x0 -> x1, Pallas kernels: none -> 2.11 us  [body(): pl.pallas_call(hand_over, out_shape=tuple((jax.ShapeDtypeStruct(x.shape,...]
where the time goes in v3:
time: 64.9 us; the launch traced here: 64.7 us
  Pallas kernels  63.9 us (98%)
  between operations  0.8 us (1%)
    pallas_call x1, Pallas kernels, body(): pl.pallas_call(functools.partial(kernel, nk, ns), out_shape=(jax.ShapeDty...  61.8 us
    pallas_call x1, Pallas kernels, body(): pl.pallas_call(hand_over, out_shape=tuple((jax.ShapeDtypeStruct(x.shape,...  2.11 us

profile of v3, /device:TPU:1, one launch (start us, length us, event | category | flops | bytes accessed | tf_op | source)
XLA Modules:
  0.0 64.7 jit_solution(17347128873567047026)
XLA Ops:
  0.6 61.8 %attend.1 = (bf16[32,8192]{1,0:T(8,128)(2,1)}, bf16[32,8192]{1,0:T(8,128)(2,1)}, bf16[32,1024]{1,0:T(8,128)(2,1)}, bf16[32,1024]{1,0:T(8,128)(2,1)}) custom-call(s32[32]{0:T(128)} %lens_ref.1, bf16[32,8192]{1,0:T(8,128)(2,1)} %q_ref.1, bf16[32,1024]{1,0:T(8,128)(2,1)} %k_ref.1, bf16[32,1024]{1,0:T(8,128)(2,1)} %v_ref.1, bf16[32,8192]{1,0:T(8,128)(2,1)} %g_ref.1), custom_call_target="tpu_custom_call" | custom-call | tf_op jit(solution)/shard_map/attend/pallas_call | solution.py:383
  62.5 2.1 %hand_over.1 = (bf16[32,8192]{1,0:T(8,128)(2,1)}, bf16[32,8192]{1,0:T(8,128)(2,1)}, bf16[32,1024]{1,0:T(8,128)(2,1)}, bf16[32,1024]{1,0:T(8,128)(2,1)}) custom-call(bf16[32,8192]{1,0:T(8,128)(2,1)} %get-tuple-element.8.refs_0_, bf16[32,8192]{1,0:T(8,128)(2,1)} %get-tuple-element.9.refs_1_, bf16[32,1024]{1,0:T(8,128)(2,1)} %get-tuple-element.10.refs_2_, ...), custom_call_target="tpu_custom_call" | custom-call | tf_op jit(solution)/shard_map/hand_over/pallas_call | solution.py:434

commit v4 on v3

--- a/solution.py
+++ b/solution.py
@@ -11,7 +11,7 @@
 GROUP = 8
 WIN = 6
 XS = 4
-CUTS = (0, 5, 8)
+CUTS = (0, 4, 8)
 MESH = pl.DeviceIdType.MESH
 SCALE = HD ** (-0.5)
 SCALE2 = SCALE * 1.4426950408889634
@@ -39,9 +39,9 @@
 
 def kernel(
     nk, ns, lens_ref, q_ref, k_ref, v_ref, g_ref, o_out, dq_out, dk_out, dv_out,
-    q_loc, g_loc, kwin, vwin, o_loc, dq_loc, part_k, part_v, held, moved, summed, final,
+    q_loc, g_loc, kwin, vwin, o_loc, dq_loc, part_k, part_v, held, final,
     bias, key_t, val_t, scores, tops, probs, dscores, over, delta, qs, gs,
-    own_sem, in_send, in_recv, win_send, win_recv, back_send, back_recv, deep_send, deep_recv, out_send, out_recv,
+    own_sem, in_send, in_recv, win_send, win_recv, back_send, back_recv, out_send, out_recv,
 ):
     me = lax.axis_index("kv")
     spot = lax.axis_index("seq")
@@ -119,35 +119,30 @@
 
     def share(a, win):
         def hop(src, i, peer):
-            return remote(src, slot(win, i), win_send.at[a, 1 if i == 7 else 0], win_recv.at[a, i], peer)
-
-        copies = {4: hop(slot(win, WIN), WIN - 4, along(XS)), 8: hop(slot(win, WIN - 4), 7, along(XS))}
-        for e in (2, 1, 3):
+            return remote(src, slot(win, i), win_send.at[a], win_recv.at[a, i], peer)
+
+        copies = {4: hop(slot(win, WIN), WIN - 4, along(XS))}
+        for e in (1, 2, 3):
             near = jnp.where(col + e >= XS, WIN - 4, WIN)
             copies[e] = hop(win.at[span(near, rows), :], WIN - e, beside(e))
-        for e in (2, 1):
-            near = jnp.where(col + e >= XS, 7, WIN - 4)
-            copies[4 + e] = hop(win.at[span(near, rows), :], WIN - 4 - e, beside(e))
+        for e in (1, 2):
+            copies[4 + e] = hop(slot(win, WIN - e), WIN - 4 - e, along(XS))
         copies[4].start()
+        return copies
+
+    def share_beside(copies):
         for e in (2, 1, 3):
             start_if(col + e < XS, copies[e])
-        return copies
 
     def relay(copies):
         copies[4].wait_recv()
-        start_if(col >= 2, copies[8])
         for e in (2, 1, 3):
             start_if(col + e >= XS, copies[e])
-        for e in (2, 1):
-            start_if(col + e < XS, copies[4 + e])
 
     def relay_deep(copies):
-        @pl.when(col >= 2)
-        def _():
-            copies[8].wait_recv()
-
-        for e in (2, 1):
-            start_if(col + e >= XS, copies[4 + e])
+        for e in (1, 2):
+            copies[e].wait_recv()
+            copies[4 + e].start()
 
     def head(h):
         return span(h, HD)
@@ -168,18 +163,21 @@
 
     arrive(got_k)
     far_k = share(0, kwin)
+    share_beside(far_k)
     arrive(got_v)
     far_v = share(1, vwin)
     relay(far_k)
-    relay(far_v)
+    share_beside(far_v)
+    relay_deep(far_k)
     arrive(got_q)
     score(WIN)
-    relay_deep(far_k)
-    relay_deep(far_v)
-    for d in (1, 2, 3, 4, 5, 6):
-        if d != 4:
+    relay(far_v)
+    for d in (4, 1, 2, 3, 5, 6):
+        if d in (3, 5, 6):
             far_k[d].wait_recv()
         score(WIN - d)
+        if d == 3:
+            relay_deep(far_v)
 
     def weight_step(h, carry):
         top = jnp.max(tops[h], axis=0, keepdims=True) * SCALE2
@@ -197,7 +195,6 @@
 
     def scale_step(h, carry):
         inv_col = jnp.broadcast_to(over[pl.ds(h, 1), :], (HD, rows)).T
-        qs[span(h, rows), :] = (q_loc[:, head(h)].astype(F32) * inv_col).astype(BF16)
         gs[span(h, rows), :] = (g_loc[:, head(h)].astype(F32) * inv_col).astype(BF16)
         return carry
 
@@ -227,53 +224,34 @@
         low = (dot(val_t[...], probs[h]) * inv).T.astype(BF16)
         o_loc[:, head(h)] = low
         delta[pl.ds(h, 1), :] = jnp.sum((gh.astype(F32) * low.astype(F32)).T, axis=0, keepdims=True)
+        inv_col = jnp.broadcast_to(inv, (HD, rows)).T
+        qs[span(h, rows), :] = (q_loc[:, head(h)].astype(F32) * inv_col).astype(BF16)
         return carry
 
     back = {}
 
     def give(a, part, b):
         d = WIN - b
-        peer = beside(-d if d <= 3 else 4 - d)
+        peer = beside(-d) if d <= 3 else along(-XS)
         copy = remote(part.at[b], held.at[a, b], back_send.at[a], back_recv.at[a, b], peer)
         copy.start()
         back[a, d] = copy
 
-    def send_on(a, i):
-        copy = remote(moved.at[a, i], held.at[a, (WIN - 4, WIN)[i]], deep_send.at[a, i], deep_recv.at[a, i], along(-XS))
-        back[a, (4, 8)[i]] = copy
-        return copy
+    def gather_up(a, part, e):
+        back[a, 4 + e].wait_recv()
+        part[WIN - e] = (part[WIN - e].astype(F32) + held[a, WIN - 4 - e].astype(F32)).astype(BF16)
+        give(a, part, WIN - e)
 
     def wrapped(e):
         return jnp.where(col + e >= XS, 1.0, 0.0)
 
-    def pass_deep(a):
-        back[a, 5].wait_recv()
-        back[a, 6].wait_recv()
-        deep = send_on(a, 1)
-
-        @pl.when(col >= 2)
-        def _():
-            moved[a, 1] = (
-                held[a, WIN - 5].astype(F32) * wrapped(1) + held[a, WIN - 6].astype(F32) * wrapped(2)
-            ).astype(BF16)
-            deep.start()
-
     def pass_on(a, part):
         total = part[WIN - 4].astype(F32)
-        for e in (1, 2):
-            total = total + held[a, WIN - 4 - e].astype(F32) * (1.0 - wrapped(e))
         for e in (1, 2, 3):
             back[a, e].wait_recv()
             total = total + held[a, WIN - e].astype(F32) * wrapped(e)
-        summed[a] = total
-
-        @pl.when(col >= 2)
-        def _():
-            back[a, 8].wait_recv()
-            summed[a] = summed[a] + held[a, WIN].astype(F32)
-
-        moved[a, 0] = summed[a].astype(BF16)
-        send_on(a, 0).start()
+        part[WIN - 4] = total.astype(BF16)
+        give(a, part, WIN - 4)
 
     def finish(a, part, factor, dst):
         total = part[WIN].astype(F32)
@@ -284,7 +262,7 @@
         final[a] = (total * factor).astype(BF16)
         spread(len(CUTS) + a, final.at[a], dst, 0, HD, HD)
 
-    order = (0, 1, 3, 4, 5, 2, 6)
+    order = (0, 1, 3, 2, 4, 5, 6)
     for b in order:
         block = slice(b * rows, (b + 1) * rows)
 
@@ -293,17 +271,16 @@
 
         acc = lax.fori_loop(0, GROUP, dv_step, jnp.zeros((rows, HD), F32), unroll=True)
         part_v[b] = acc.astype(BF16)
-        if b < WIN and b != WIN - 4:
+        if b in (0, 1, 3):
             give(1, part_v, b)
 
-    for d in (1, 2, 3, 5, 6):
+    for d in (3, 5, 6):
         far_v[d].wait_recv()
     for b in range(WIN + 1):
         block = slice(b * rows, (b + 1) * rows)
         val_t[:, block] = vwin[block].T
     lax.fori_loop(0, GROUP, out_step, 0, unroll=2)
     spread(0, o_loc, o_out, 0, width, width)
-    pass_deep(1)
 
     for b in order:
         block = slice(b * rows, (b + 1) * rows)
@@ -317,13 +294,15 @@
 
         acc = lax.fori_loop(0, GROUP, dk_step, jnp.zeros((rows, HD), F32), unroll=True)
         part_k[b] = acc.astype(BF16)
-        if b < WIN and b != WIN - 4:
+        if b in (0, 1, 3):
             give(0, part_k, b)
-        if b == 1:
+        if b == 0:
+            gather_up(1, part_v, 2)
+            gather_up(1, part_v, 1)
+        if b in (4, 5):
+            gather_up(0, part_k, WIN - b)
+        if b == 5:
             pass_on(1, part_v)
-        if b == 2:
-            pass_deep(0)
-    finish(1, part_v, 1.0, dv_out)
 
     def dq_step(h, carry):
         dq_t = dot(key_t[...], dscores[h])
@@ -338,23 +317,17 @@
         spread(1 + i, dq_loc, dq_out, low * HD, (high - low) * HD, width)
         if i == 0:
             pass_on(0, part_k)
+            finish(1, part_v, 1.0, dv_out)
     finish(0, part_k, SCALE, dk_out)
 
     for copy in leaving:
         copy.wait_send()
     for a, win in enumerate((kwin, vwin)):
         six = win.at[pl.ds(0, WIN * rows), :]
-        remote(six, six, win_send.at[a, 0], win_recv.at[a, 0], along(XS)).wait_send()
+        remote(six, six, win_send.at[a], win_recv.at[a, 0], along(XS)).wait_send()
     for a, part in enumerate((part_k, part_v)):
-        five = part.at[pl.ds(0, WIN - 1)]
-        remote(five, five, back_send.at[a], back_recv.at[a, 0], along(XS)).wait_send()
-        back[a, 4].wait_send()
-
-    @pl.when(col >= 2)
-    def _():
-        for copy in (far_k[8], far_v[8], back[0, 8], back[1, 8]):
-            copy.wait_send()
-
+        six = part.at[pl.ds(0, WIN)]
+        remote(six, six, back_send.at[a], back_recv.at[a, 0], along(XS)).wait_send()
     for copy in pending:
         copy.wait()
 
@@ -393,15 +366,13 @@
         scratch_shapes=[
             pltpu.VMEM((rows, width), BF16),
             pltpu.VMEM((rows, width), BF16),
-            pltpu.VMEM(((blocks + 1) * rows, HD), BF16),
-            pltpu.VMEM(((blocks + 1) * rows, HD), BF16),
+            pltpu.VMEM((blocks * rows, HD), BF16),
+            pltpu.VMEM((blocks * rows, HD), BF16),
             pltpu.VMEM((rows, width), BF16),
             pltpu.VMEM((rows, width), BF16),
             pltpu.VMEM((blocks, rows, HD), BF16),
             pltpu.VMEM((blocks, rows, HD), BF16),
             pltpu.VMEM((2, blocks, rows, HD), BF16),
-            pltpu.VMEM((2, 2, rows, HD), BF16),
-            pltpu.VMEM((2, rows, HD), F32),
             pltpu.VMEM((2, rows, HD), BF16),
             pltpu.VMEM((blocks, rows, rows), F32),
             pltpu.VMEM((HD, blocks * rows), BF16),
@@ -417,12 +388,10 @@
             dma((4 + len(CUTS) + 2,)),
             dma((4,)),
             dma((4,)),
-            dma((2, 2)),
-            dma((2, 8)),
             dma((2,)),
             dma((2, blocks)),
-            dma((2, 2)),
-            dma((2, 2)),
+            dma((2,)),
+            dma((2, blocks)),
             dma((len(CUTS) + 2,)),
             dma((len(CUTS) + 2,)),
         ],

time: 64.9 us -> 61.3 us (0.945)
  Pallas kernels: 63.9 us -> 60.3 us
    pallas_call x1, Pallas kernels: 61.8 us -> 58.2 us  [body(): pl.pallas_call(functools.partial(kernel, nk, ns), out_shape=(jax.ShapeDty...]
where the time goes in v4:
time: 61.3 us; the launch traced here: 61.1 us
  Pallas kernels  60.3 us (98%)
  between operations  0.8 us (1%)
    pallas_call x1, Pallas kernels, body(): pl.pallas_call(functools.partial(kernel, nk, ns), out_shape=(jax.ShapeDty...  58.2 us
    pallas_call x1, Pallas kernels, body(): pl.pallas_call(hand_over, out_shape=tuple((jax.ShapeDtypeStruct(x.shape,...  2.11 us

profile of v4, /device:TPU:1, one launch (start us, length us, event | category | flops | bytes accessed | tf_op | source)
XLA Modules:
  0.0 61.1 jit_solution(12973446844258316149)
XLA Ops:
  0.6 58.2 %attend.1 = (bf16[32,8192]{1,0:T(8,128)(2,1)}, bf16[32,8192]{1,0:T(8,128)(2,1)}, bf16[32,1024]{1,0:T(8,128)(2,1)}, bf16[32,1024]{1,0:T(8,128)(2,1)}) custom-call(s32[32]{0:T(128)} %lens_ref.1, bf16[32,8192]{1,0:T(8,128)(2,1)} %q_ref.1, bf16[32,1024]{1,0:T(8,128)(2,1)} %k_ref.1, bf16[32,1024]{1,0:T(8,128)(2,1)} %v_ref.1, bf16[32,8192]{1,0:T(8,128)(2,1)} %g_ref.1), custom_call_target="tpu_custom_call" | custom-call | tf_op jit(solution)/shard_map/attend/pallas_call | solution.py:356
  58.8 2.1 %hand_over.1 = (bf16[32,8192]{1,0:T(8,128)(2,1)}, bf16[32,8192]{1,0:T(8,128)(2,1)}, bf16[32,1024]{1,0:T(8,128)(2,1)}, bf16[32,1024]{1,0:T(8,128)(2,1)}) custom-call(bf16[32,8192]{1,0:T(8,128)(2,1)} %get-tuple-element.8.refs_0_, bf16[32,8192]{1,0:T(8,128)(2,1)} %get-tuple-element.9.refs_1_, bf16[32,1024]{1,0:T(8,128)(2,1)} %get-tuple-element.10.refs_2_, ...), custom_call_target="tpu_custom_call" | custom-call | tf_op jit(solution)/shard_map/hand_over/pallas_call | solution.py:403

commit v5 on v4

--- a/solution.py
+++ b/solution.py
@@ -40,7 +40,7 @@
 def kernel(
     nk, ns, lens_ref, q_ref, k_ref, v_ref, g_ref, o_out, dq_out, dk_out, dv_out,
     q_loc, g_loc, kwin, vwin, o_loc, dq_loc, part_k, part_v, held, final,
-    bias, key_t, val_t, scores, tops, probs, dscores, over, delta, qs, gs,
+    bias, key_t, val_t, scores, tops, probs, dscores, over, delta, qs, sum_v,
     own_sem, in_send, in_recv, win_send, win_recv, back_send, back_recv, out_send, out_recv,
 ):
     me = lax.axis_index("kv")
@@ -49,7 +49,7 @@
     tok = q_ref.shape[0]
     rows = tok * nk
     width = GROUP * HD
-    peers = [lax.rem(me + o, nk) for o in range(1, nk)]
+    peers = [lax.rem(me + o, nk) for o in sorted(range(1, nk), key=lambda o: abs(o - nk // 2))]
 
     def along(d):
         return {"seq": lax.rem(spot + ns + d, ns)}
@@ -179,27 +179,6 @@
         if d == 3:
             relay_deep(far_v)
 
-    def weight_step(h, carry):
-        top = jnp.max(tops[h], axis=0, keepdims=True) * SCALE2
-        total = jnp.zeros((8, rows), F32)
-        for b in range(WIN + 1):
-            block = slice(b * rows, (b + 1) * rows)
-            p = jnp.exp2(scores[h, block] * SCALE2 - top)
-            total = total + fold(p, jnp.sum)
-            probs[h, block] = p.astype(BF16)
-        over[pl.ds(h, 1), :] = 1.0 / jnp.sum(total, axis=0, keepdims=True)
-        return carry
-
-    lax.fori_loop(0, GROUP, weight_step, 0)
-    arrive(got_g)
-
-    def scale_step(h, carry):
-        inv_col = jnp.broadcast_to(over[pl.ds(h, 1), :], (HD, rows)).T
-        gs[span(h, rows), :] = (g_loc[:, head(h)].astype(F32) * inv_col).astype(BF16)
-        return carry
-
-    lax.fori_loop(0, GROUP, scale_step, 0, unroll=2)
-
     def spread(a, src, dst, base, size, wide):
         def rows_of(to):
             return src.at[span(to, tok), pl.ds(base, size)]
@@ -262,17 +241,33 @@
         final[a] = (total * factor).astype(BF16)
         spread(len(CUTS) + a, final.at[a], dst, 0, HD, HD)
 
-    order = (0, 1, 3, 2, 4, 5, 6)
-    for b in order:
-        block = slice(b * rows, (b + 1) * rows)
-
-        def dv_step(h, acc):
-            return acc + dot(probs[h, block], gs[span(h, rows), :])
-
-        acc = lax.fori_loop(0, GROUP, dv_step, jnp.zeros((rows, HD), F32), unroll=True)
-        part_v[b] = acc.astype(BF16)
-        if b in (0, 1, 3):
-            give(1, part_v, b)
+    order = (0, 1, 3, 4, 5, 2, 6)
+    arrive(got_g)
+    for h in range(GROUP + 1):
+        if h < GROUP:
+            top = jnp.max(tops[h], axis=0, keepdims=True) * SCALE2
+            total = jnp.zeros((8, rows), F32)
+        if h > 0:
+            inv_col = jnp.broadcast_to(over[h - 1:h, :], (HD, rows)).T
+            gh = (g_loc[:, (h - 1) * HD:h * HD].astype(F32) * inv_col).astype(BF16)
+        for b in range(WIN + 1):
+            block = slice(b * rows, (b + 1) * rows)
+            if h < GROUP:
+                p = jnp.exp2(scores[h, block] * SCALE2 - top)
+                total = total + fold(p, jnp.sum)
+                probs[h, block] = p.astype(BF16)
+            if h > 0:
+                acc = dot(probs[h - 1, block], gh)
+                if h > 1:
+                    acc = acc + sum_v[b]
+                if h < GROUP:
+                    sum_v[b] = acc
+                else:
+                    part_v[b] = acc.astype(BF16)
+        if h < GROUP:
+            over[h:h + 1, :] = 1.0 / jnp.sum(total, axis=0, keepdims=True)
+    for b in (0, 1, 3):
+        give(1, part_v, b)
 
     for d in (3, 5, 6):
         far_v[d].wait_recv()
@@ -301,7 +296,7 @@
             gather_up(1, part_v, 1)
         if b in (4, 5):
             gather_up(0, part_k, WIN - b)
-        if b == 5:
+        if b == 2:
             pass_on(1, part_v)
 
     def dq_step(h, carry):
@@ -317,7 +312,7 @@
         spread(1 + i, dq_loc, dq_out, low * HD, (high - low) * HD, width)
         if i == 0:
             pass_on(0, part_k)
-            finish(1, part_v, 1.0, dv_out)
+    finish(1, part_v, 1.0, dv_out)
     finish(0, part_k, SCALE, dk_out)
 
     for copy in leaving:
@@ -384,7 +379,7 @@
             pltpu.VMEM((GROUP, rows), F32),
             pltpu.VMEM((GROUP, rows), F32),
             pltpu.VMEM((GROUP * rows, HD), BF16),
-            pltpu.VMEM((GROUP * rows, HD), BF16),
+            pltpu.VMEM((blocks, rows, HD), F32),
             dma((4 + len(CUTS) + 2,)),
             dma((4,)),
             dma((4,)),

time: 61.3 us -> 60.3 us (0.984)
  Pallas kernels: 60.3 us -> 59.3 us
    pallas_call x1, Pallas kernels: 58.2 us -> 57.2 us  [body(): pl.pallas_call(functools.partial(kernel, nk, ns), out_shape=(jax.ShapeDty...]
where the time goes in v5:
time: 60.3 us; the launch traced here: 60.1 us
  Pallas kernels  59.3 us (98%)
  between operations  0.8 us (1%)
    pallas_call x1, Pallas kernels, body(): pl.pallas_call(functools.partial(kernel, nk, ns), out_shape=(jax.ShapeDty...  57.2 us
    pallas_call x1, Pallas kernels, body(): pl.pallas_call(hand_over, out_shape=tuple((jax.ShapeDtypeStruct(x.shape,...  2.11 us

profile of v5, /device:TPU:1, one launch (start us, length us, event | category | flops | bytes accessed | tf_op | source)
XLA Modules:
  0.0 60.1 jit_solution(15589490250181579940)
XLA Ops:
  0.6 57.2 %attend.1 = (bf16[32,8192]{1,0:T(8,128)(2,1)}, bf16[32,8192]{1,0:T(8,128)(2,1)}, bf16[32,1024]{1,0:T(8,128)(2,1)}, bf16[32,1024]{1,0:T(8,128)(2,1)}) custom-call(s32[32]{0:T(128)} %lens_ref.1, bf16[32,8192]{1,0:T(8,128)(2,1)} %q_ref.1, bf16[32,1024]{1,0:T(8,128)(2,1)} %k_ref.1, bf16[32,1024]{1,0:T(8,128)(2,1)} %v_ref.1, bf16[32,8192]{1,0:T(8,128)(2,1)} %g_ref.1), custom_call_target="tpu_custom_call" | custom-call | tf_op jit(solution)/shard_map/attend/pallas_call | solution.py:351
  57.8 2.1 %hand_over.1 = (bf16[32,8192]{1,0:T(8,128)(2,1)}, bf16[32,8192]{1,0:T(8,128)(2,1)}, bf16[32,1024]{1,0:T(8,128)(2,1)}, bf16[32,1024]{1,0:T(8,128)(2,1)}) custom-call(bf16[32,8192]{1,0:T(8,128)(2,1)} %get-tuple-element.8.refs_0_, bf16[32,8192]{1,0:T(8,128)(2,1)} %get-tuple-element.9.refs_1_, bf16[32,1024]{1,0:T(8,128)(2,1)} %get-tuple-element.10.refs_2_, ...), custom_call_target="tpu_custom_call" | custom-call | tf_op jit(solution)/shard_map/hand_over/pallas_call | solution.py:398

commit v6 on v5

--- a/solution.py
+++ b/solution.py
@@ -168,10 +168,10 @@
     far_v = share(1, vwin)
     relay(far_k)
     share_beside(far_v)
+    relay(far_v)
     relay_deep(far_k)
     arrive(got_q)
     score(WIN)
-    relay(far_v)
     for d in (4, 1, 2, 3, 5, 6):
         if d in (3, 5, 6):
             far_k[d].wait_recv()
@@ -274,7 +274,7 @@
     for b in range(WIN + 1):
         block = slice(b * rows, (b + 1) * rows)
         val_t[:, block] = vwin[block].T
-    lax.fori_loop(0, GROUP, out_step, 0, unroll=2)
+    lax.fori_loop(0, GROUP, out_step, 0, unroll=4)
     spread(0, o_loc, o_out, 0, width, width)
 
     for b in order:
@@ -309,11 +309,11 @@
         key_t[:, block] = kwin[block].T
     for i, (low, high) in enumerate(zip(CUTS, CUTS[1:])):
         lax.fori_loop(low, high, dq_step, 0, unroll=True)
-        spread(1 + i, dq_loc, dq_out, low * HD, (high - low) * HD, width)
         if i == 0:
             pass_on(0, part_k)
+        spread(1 + i, dq_loc, dq_out, low * HD, (high - low) * HD, width)
+    finish(0, part_k, SCALE, dk_out)
     finish(1, part_v, 1.0, dv_out)
-    finish(0, part_k, SCALE, dk_out)
 
     for copy in leaving:
         copy.wait_send()

time: 60.3 us -> 60.3 us (level)
  no operation moved by 1% of the time
where the time goes in v6:
time: 60.3 us; the launch traced here: 60.1 us
  Pallas kernels  59.3 us (98%)
  between operations  0.8 us (1%)
    pallas_call x1, Pallas kernels, body(): pl.pallas_call(functools.partial(kernel, nk, ns), out_shape=(jax.ShapeDty...  57.2 us
    pallas_call x1, Pallas kernels, body(): pl.pallas_call(hand_over, out_shape=tuple((jax.ShapeDtypeStruct(x.shape,...  2.11 us

profile of v6, /device:TPU:1, one launch (start us, length us, event | category | flops | bytes accessed | tf_op | source)
XLA Modules:
  0.0 60.1 jit_solution(15349520360541380348)
XLA Ops:
  0.6 57.2 %attend.1 = (bf16[32,8192]{1,0:T(8,128)(2,1)}, bf16[32,8192]{1,0:T(8,128)(2,1)}, bf16[32,1024]{1,0:T(8,128)(2,1)}, bf16[32,1024]{1,0:T(8,128)(2,1)}) custom-call(s32[32]{0:T(128)} %lens_ref.1, bf16[32,8192]{1,0:T(8,128)(2,1)} %q_ref.1, bf16[32,1024]{1,0:T(8,128)(2,1)} %k_ref.1, bf16[32,1024]{1,0:T(8,128)(2,1)} %v_ref.1, bf16[32,8192]{1,0:T(8,128)(2,1)} %g_ref.1), custom_call_target="tpu_custom_call" | custom-call | tf_op jit(solution)/shard_map/attend/pallas_call | solution.py:351
  57.9 2.1 %hand_over.1 = (bf16[32,8192]{1,0:T(8,128)(2,1)}, bf16[32,8192]{1,0:T(8,128)(2,1)}, bf16[32,1024]{1,0:T(8,128)(2,1)}, bf16[32,1024]{1,0:T(8,128)(2,1)}) custom-call(bf16[32,8192]{1,0:T(8,128)(2,1)} %get-tuple-element.8.refs_0_, bf16[32,8192]{1,0:T(8,128)(2,1)} %get-tuple-element.9.refs_1_, bf16[32,1024]{1,0:T(8,128)(2,1)} %get-tuple-element.10.refs_2_, ...), custom_call_target="tpu_custom_call" | custom-call | tf_op jit(solution)/shard_map/hand_over/pallas_call | solution.py:398
